TPU v7x, 32 devices: a whole 2x2x4 slice. The times are simulated.
32 devices in a mesh: dp: 4 (over y, x), expert: 8 (over z, core).
Axes of the slice: x: 2, y: 2, z: 4, core: 2. Of those that a mesh axis runs over, the one named last changes fastest.
Arguments:
- tokens: bfloat16 [32768, 768], P(('dp', 'expert')), may hold values from -6 to 6
- cotangent: bfloat16 [32768, 768], P(('dp', 'expert')), may hold values from -6 to 6
- lengths: int32 [64, 3], P(('dp', 'expert')), may hold values from 1 to 384, 512 in all within a row
- routes: int32 [32768, 1], P(('dp', 'expert')), may hold values from 0 to 15; in each aligned block of 512 rows (0 to 511, 512 to 1023, ...) at most 64 rows name the same one
- w_query: bfloat16 [768, 768], P(('dp', 'expert')), may hold values from -0.21875 to 0.21875
- w_key: bfloat16 [768, 768], P(('dp', 'expert')), may hold values from -0.21875 to 0.21875
- w_value: bfloat16 [768, 768], P(('dp', 'expert')), may hold values from -0.21875 to 0.21875
- w_output: bfloat16 [768, 768], P(('dp', 'expert')), may hold values from -1.25 to 1.25
- router: bfloat16 [768, 16], P(('dp', 'expert')), may hold values from -0.109375 to 0.109375
- gain_first: bfloat16 [768], P(('dp', 'expert')), may hold values from 0.5 to 1.5
- gain_second: bfloat16 [768], P(('dp', 'expert')), may hold values from 0.5 to 1.5
- bias_table: float32 [32, 12], replicated, may hold values from -4 to 4
- w_in: bfloat16 [16, 768, 3072], P('expert', None, 'dp'), may hold values from -0.21875 to 0.21875
- w_out: bfloat16 [16, 3072, 768], P('expert', 'dp')
Outputs:
- block_out: bfloat16 [32768, 768], P(('dp', 'expert'))
- grad_tokens: float32 [32768, 768], P(('dp', 'expert'))
- grad_query: float32 [768, 768], P(('dp', 'expert'))
- grad_key: float32 [768, 768], P(('dp', 'expert'))
- grad_value: float32 [768, 768], P(('dp', 'expert'))
- grad_output: float32 [768, 768], P(('dp', 'expert'))
- grad_router: float32 [768, 16], P(('dp', 'expert'))
- grad_gain_first: float32 [768], P(('dp', 'expert'))
- grad_gain_second: float32 [768], P(('dp', 'expert'))
- grad_bias_table: float32 [32, 12], replicated
- grad_in: float32 [16, 768, 3072], P('expert', None, 'dp')
- grad_out: float32 [16, 3072, 768], P('expert', 'dp')
Inputs may be any that keep to these rules, and one draw needn't show every extreme that they name: Each row holds the lengths of the sequences of one micro-batch block, in order; they sum to 512. `routes`: within each micro-batch block (8 on the larger slice: 2 * 512 / experts) of 512 rows of one device, no expert is named by more than 64 tokens.
All inputs are finite; a program needn't handle non-finite values.
Results may differ from a plain program's by a relative error of at most 0.023.
Values may be sent and summed in bfloat16 or wider, within the bound.
A program may use at most 320 MiB of HBM per device.

v0:
```python
import jax
import jax.numpy as jnp
from jax import lax
from jax.sharding import PartitionSpec as P

H = 12
HD = 64


EPSILON = 1e-06
THRESHOLDS = (12, 16, 23, 32, 46, 64, 91)
NEGATIVE = -1e30


def bucket_grid(extent):
    places = jnp.arange(extent, dtype=jnp.int32)
    offset = places[None, :] - places[:, None]
    spread = jnp.abs(offset)
    beyond = 8 + sum(((spread >= threshold).astype(jnp.int32) for threshold in THRESHOLDS))
    return jnp.where(offset > 0, 16, 0).astype(jnp.int32) + jnp.where(spread < 8, spread, beyond)


def same_sequence(seq_lengths, extent):
    places = jnp.arange(extent, dtype=jnp.int32)
    ending = jnp.cumsum(seq_lengths)
    segment = jnp.sum((places[:, None] >= ending[None, :]).astype(jnp.int32), axis=1)
    return segment[:, None] == segment[None, :]


def gelu_tanh(values):
    return jax.nn.gelu(values, approximate=True)


def rms_forward(values, gain_vector):
    scale_row = lax.rsqrt(jnp.mean(values * values, axis=-1, keepdims=True) + EPSILON)
    return (scale_row, values * scale_row * gain_vector)


def rms_backward(values, scale_row, gain_vector, grad_scaled):
    weighted = grad_scaled * gain_vector
    grad_values = scale_row * weighted - values * scale_row**3 * jnp.mean(
        weighted * values, axis=-1, keepdims=True
    )
    grad_gain = jnp.sum(grad_scaled * values * scale_row, axis=0)
    return (grad_values, grad_gain)


def contract_rows(former, latter):
    return lax.dot_general(
        former, latter, (((0,), (0,)), ((), ())), preferred_element_type=jnp.float32
    )


def contract_cols(former, latter):
    return lax.dot_general(
        former, latter, (((1,), (1,)), ((), ())), preferred_element_type=jnp.float32
    )


def masked_scores(query_rows, keys_block, bias_grid, allowed):
    extent = query_rows.shape[0]
    scores = jnp.einsum(
        "phd,qhd->hpq",
        query_rows.reshape(extent, H, HD),
        keys_block.reshape(extent, H, HD),
        preferred_element_type=jnp.float32,
    )
    scores = scores * HD ** (-0.5) + bias_grid
    return jnp.where(allowed[None], scores, NEGATIVE)


def attention_forward(query_rows, keys_block, values_block, bias_grid, allowed):
    extent = query_rows.shape[0]
    masked = masked_scores(query_rows, keys_block, bias_grid, allowed)
    row_peak = jnp.max(masked, axis=-1, keepdims=True)
    log_total = row_peak + jnp.log(jnp.sum(jnp.exp(masked - row_peak), axis=-1, keepdims=True))
    soft_low = jnp.exp(masked - log_total).astype(jnp.bfloat16)
    context = jnp.einsum(
        "hpq,qhd->phd",
        soft_low,
        values_block.reshape(extent, H, HD),
        preferred_element_type=jnp.float32,
    )
    return (context.reshape(extent, H * HD).astype(jnp.bfloat16), log_total)


def attention_backward(
    query_rows, keys_block, values_block, bias_grid, allowed, log_total, grad_context, bucket_half
):
    extent = query_rows.shape[0]
    soft_weights = jnp.exp(masked_scores(query_rows, keys_block, bias_grid, allowed) - log_total)
    soft_low = soft_weights.astype(jnp.bfloat16)
    grad_heads = grad_context.reshape(extent, H, HD)
    grad_soft = jnp.einsum(
        "phd,qhd->hpq",
        grad_heads,
        values_block.reshape(extent, H, HD),
        preferred_element_type=jnp.float32,
    )
    grad_value = (
        jnp.einsum("hpq,phd->qhd", soft_low, grad_heads, preferred_element_type=jnp.float32)
        .reshape(extent, H * HD)
        .astype(jnp.bfloat16)
    )
    inner = jnp.sum(grad_soft * soft_weights, axis=-1, keepdims=True)
    grad_scores = (soft_weights * (grad_soft - inner)).astype(jnp.bfloat16)
    grad_query = jnp.einsum(
        "hpq,qhd->phd",
        grad_scores,
        keys_block.reshape(extent, H, HD),
        preferred_element_type=jnp.float32,
    ) * HD ** (-0.5)
    grad_key = jnp.einsum(
        "hpq,phd->qhd",
        grad_scores,
        query_rows.reshape(extent, H, HD),
        preferred_element_type=jnp.float32,
    ) * HD ** (-0.5)
    grad_table = lax.dot_general(
        bucket_half,
        grad_scores.reshape(H, extent * extent),
        (((1,), (1,)), ((), ())),
        preferred_element_type=jnp.float32,
    )
    return (
        grad_query.reshape(extent, H * HD).astype(jnp.bfloat16),
        grad_key.reshape(extent, H * HD).astype(jnp.bfloat16),
        grad_value,
        grad_table,
    )


def local(
    tokens,
    cotangent,
    lengths,
    routes,
    w_query,
    w_key,
    w_value,
    w_output,
    router,
    gain_first,
    gain_second,
    bias_table,
    w_in,
    w_out,
):
    micro_count = lengths.shape[0]
    block_rows = tokens.shape[0] // micro_count
    model_width = tokens.shape[1]
    expert_local = w_in.shape[0]
    expert_total = expert_local * lax.axis_size("expert")
    capacity = 2 * block_rows // expert_total
    bucket_count = bias_table.shape[0]
    bucket_flat = bucket_grid(block_rows).reshape(1, block_rows * block_rows)
    bucket_float = (jnp.arange(bucket_count, dtype=jnp.int32)[:, None] == bucket_flat).astype(
        jnp.float32
    )
    bias_grid = lax.dot_general(
        bias_table,
        bucket_float,
        (((0,), (0,)), ((), ())),
        precision=lax.Precision.HIGHEST,
        preferred_element_type=jnp.float32,
    ).reshape(H, block_rows, block_rows)
    bucket_half = bucket_float.astype(jnp.bfloat16)
    expert_iota = jnp.arange(expert_total, dtype=jnp.int32)
    dense_parts = (w_query, w_key, w_value, w_output, router, gain_first, gain_second)
    full_in, full_out = (w_in, w_out)
    stored = []
    out_blocks = []
    for micro_index in range(micro_count):
        row_start = micro_index * block_rows
        gathered = (
            lax.all_gather(dense_parts[0], ("dp", "expert"), axis=0, tiled=True),
            lax.all_gather(dense_parts[1], ("dp", "expert"), axis=0, tiled=True),
            lax.all_gather(dense_parts[2], ("dp", "expert"), axis=0, tiled=True),
            lax.all_gather(dense_parts[3], ("dp", "expert"), axis=0, tiled=True),
            lax.all_gather(dense_parts[4], ("dp", "expert"), axis=0, tiled=True),
            lax.all_gather(dense_parts[5], ("dp", "expert"), axis=0, tiled=True),
            lax.all_gather(dense_parts[6], ("dp", "expert"), axis=0, tiled=True),
        )
        query_weight, key_weight, value_weight, output_weight, router_full, gain_one, gain_two = (
            gathered
        )
        rows_in = tokens[row_start : row_start + block_rows].astype(jnp.float32)
        scale_one, scaled_one = rms_forward(rows_in, gain_one.astype(jnp.float32))
        normed = scaled_one.astype(jnp.bfloat16)
        query_rows = jnp.dot(normed, query_weight, preferred_element_type=jnp.float32).astype(
            jnp.bfloat16
        )
        keys_block = jnp.dot(normed, key_weight, preferred_element_type=jnp.float32).astype(
            jnp.bfloat16
        )
        values_block = jnp.dot(normed, value_weight, preferred_element_type=jnp.float32).astype(
            jnp.bfloat16
        )
        allowed = same_sequence(lengths[micro_index], block_rows)
        context, log_total = attention_forward(
            query_rows, keys_block, values_block, bias_grid, allowed
        )
        middle = rows_in + jnp.dot(context, output_weight, preferred_element_type=jnp.float32)
        scale_two, scaled_two = rms_forward(middle, gain_two.astype(jnp.float32))
        second = scaled_two.astype(jnp.bfloat16)
        logits = jnp.dot(second, router_full, preferred_element_type=jnp.float32)
        row_peak = jnp.max(logits, axis=-1, keepdims=True)
        exps = jnp.exp(logits - row_peak)
        gate_probs = exps / jnp.sum(exps, axis=-1, keepdims=True)
        route_now = routes[row_start : row_start + block_rows, 0]
        choose = (route_now[:, None] == expert_iota[None, :]).astype(jnp.int32)
        slot_index = jnp.sum(jnp.cumsum(choose, axis=0) * choose, axis=-1) - 1
        row_index = route_now * capacity + slot_index
        choose_float = choose.astype(jnp.float32)
        gate_value = jnp.sum(gate_probs * choose_float, axis=-1)
        buffer = (
            jnp.zeros((expert_total * capacity, model_width), jnp.bfloat16)
            .at[row_index]
            .set(second)
        )
        received = lax.all_to_all(
            buffer.reshape(expert_total, capacity, model_width),
            "expert",
            split_axis=0,
            concat_axis=1,
            tiled=True,
        )
        expert_rows = lax.all_gather(received, "dp", axis=1, tiled=True)
        expert_pre = jnp.einsum(
            "erd,edf->erf", expert_rows, w_in, preferred_element_type=jnp.float32
        )
        hidden = gelu_tanh(expert_pre).astype(jnp.bfloat16)
        partial_value = jnp.einsum(
            "erf,efd->erd", hidden, w_out, preferred_element_type=jnp.float32
        )
        expert_sum = lax.psum_scatter(
            partial_value.astype(jnp.bfloat16), "dp", scatter_dimension=1, tiled=True
        )
        returned = lax.all_to_all(expert_sum, "expert", split_axis=1, concat_axis=0, tiled=True)
        expert_out = returned.reshape(expert_total * capacity, model_width)[row_index].astype(
            jnp.float32
        )
        out_blocks.append((middle + gate_value[:, None] * expert_out).astype(jnp.bfloat16))
        stored.append(
            {
                "weights": gathered,
                "rows_in": rows_in,
                "scale_one": scale_one,
                "normed": normed,
                "query_rows": query_rows,
                "keys_block": keys_block,
                "values_block": values_block,
                "allowed": allowed,
                "context": context,
                "log_total": log_total,
                "middle": middle,
                "scale_two": scale_two,
                "second": second,
                "gate_probs": gate_probs,
                "choose_float": choose_float,
                "row_index": row_index,
                "gate_value": gate_value,
                "expert_rows": expert_rows,
                "expert_pre": expert_pre,
                "hidden": hidden,
                "expert_out": expert_out,
            }
        )
    total_query = jnp.zeros((model_width, model_width), jnp.float32)
    total_key = jnp.zeros((model_width, model_width), jnp.float32)
    total_value = jnp.zeros((model_width, model_width), jnp.float32)
    total_output = jnp.zeros((model_width, model_width), jnp.float32)
    total_router = jnp.zeros((model_width, expert_total), jnp.float32)
    total_gain_one = jnp.zeros((model_width,), jnp.float32)
    total_gain_two = jnp.zeros((model_width,), jnp.float32)
    total_table = jnp.zeros(bias_table.shape, jnp.float32)
    total_in = jnp.zeros(full_in.shape, jnp.float32)
    total_out = jnp.zeros(full_out.shape, jnp.float32)
    grad_blocks = [None] * micro_count
    for micro_index in reversed(range(micro_count)):
        kept = stored[micro_index]
        row_start = micro_index * block_rows
        gathered = (
            lax.all_gather(dense_parts[0], ("dp", "expert"), axis=0, tiled=True),
            lax.all_gather(dense_parts[1], ("dp", "expert"), axis=0, tiled=True),
            lax.all_gather(dense_parts[2], ("dp", "expert"), axis=0, tiled=True),
            lax.all_gather(dense_parts[3], ("dp", "expert"), axis=0, tiled=True),
            lax.all_gather(dense_parts[4], ("dp", "expert"), axis=0, tiled=True),
            lax.all_gather(dense_parts[5], ("dp", "expert"), axis=0, tiled=True),
            lax.all_gather(dense_parts[6], ("dp", "expert"), axis=0, tiled=True),
        )
        query_weight, key_weight, value_weight, output_weight, router_full, gain_one, gain_two = (
            gathered
        )
        grad_final = cotangent[row_start : row_start + block_rows].astype(jnp.float32)
        grad_gate = jnp.sum(grad_final * kept["expert_out"], axis=-1)
        grad_expert = (kept["gate_value"][:, None] * grad_final).astype(jnp.bfloat16)
        buffer = (
            jnp.zeros((expert_total * capacity, model_width), jnp.bfloat16)
            .at[kept["row_index"]]
            .set(grad_expert)
        )
        grad_received = lax.all_to_all(
            buffer.reshape(expert_total, capacity, model_width),
            "expert",
            split_axis=0,
            concat_axis=1,
            tiled=True,
        )
        grad_rows = lax.all_gather(grad_received, "dp", axis=1, tiled=True)
        grad_hidden = jnp.einsum(
            "erd,efd->erf", grad_rows, full_out, preferred_element_type=jnp.float32
        )
        gelu_value, gelu_pull = jax.vjp(gelu_tanh, kept["expert_pre"])
        grad_pre = gelu_pull(grad_hidden)[0].astype(jnp.bfloat16)
        total_out = total_out + jnp.einsum(
            "erf,erd->efd", kept["hidden"], grad_rows, preferred_element_type=jnp.float32
        )
        total_in = total_in + jnp.einsum(
            "erd,erf->edf", kept["expert_rows"], grad_pre, preferred_element_type=jnp.float32
        )
        partial_back = jnp.einsum(
            "erf,edf->erd", grad_pre, full_in, preferred_element_type=jnp.float32
        )
        grad_sent = lax.psum_scatter(
            partial_back.astype(jnp.bfloat16), "dp", scatter_dimension=1, tiled=True
        )
        grad_returned = lax.all_to_all(grad_sent, "expert", split_axis=1, concat_axis=0, tiled=True)
        grad_second = grad_returned.reshape(expert_total * capacity, model_width)[
            kept["row_index"]
        ].astype(jnp.float32)
        gate_probs = kept["gate_probs"]
        grad_logits = gate_probs * (
            kept["choose_float"] * grad_gate[:, None] - (kept["gate_value"] * grad_gate)[:, None]
        )
        grad_logits = grad_logits.astype(jnp.bfloat16)
        total_router = total_router + contract_rows(kept["second"], grad_logits)
        grad_second = grad_second + contract_cols(grad_logits, router_full)
        grad_part, grad_gain = rms_backward(
            kept["middle"], kept["scale_two"], gain_two.astype(jnp.float32), grad_second
        )
        total_gain_two = total_gain_two + grad_gain
        grad_middle = grad_final + grad_part
        grad_attended = grad_middle.astype(jnp.bfloat16)
        total_output = total_output + contract_rows(kept["context"], grad_attended)
        grad_context = contract_cols(grad_attended, output_weight).astype(jnp.bfloat16)
        grad_query, grad_key, grad_value, grad_table = attention_backward(
            kept["query_rows"],
            kept["keys_block"],
            kept["values_block"],
            bias_grid,
            kept["allowed"],
            kept["log_total"],
            grad_context,
            bucket_half,
        )
        total_table = total_table + grad_table
        total_query = total_query + contract_rows(kept["normed"], grad_query)
        total_key = total_key + contract_rows(kept["normed"], grad_key)
        total_value = total_value + contract_rows(kept["normed"], grad_value)
        grad_normed = (
            contract_cols(grad_query, query_weight)
            + contract_cols(grad_key, key_weight)
            + contract_cols(grad_value, value_weight)
        )
        grad_part, grad_gain = rms_backward(
            kept["rows_in"], kept["scale_one"], gain_one.astype(jnp.float32), grad_normed
        )
        total_gain_one = total_gain_one + grad_gain
        grad_blocks[micro_index] = grad_middle + grad_part
    dense_shares = (
        lax.psum_scatter(total_query, ("dp", "expert"), scatter_dimension=0, tiled=True),
        lax.psum_scatter(total_key, ("dp", "expert"), scatter_dimension=0, tiled=True),
        lax.psum_scatter(total_value, ("dp", "expert"), scatter_dimension=0, tiled=True),
        lax.psum_scatter(total_output, ("dp", "expert"), scatter_dimension=0, tiled=True),
        lax.psum_scatter(total_router, ("dp", "expert"), scatter_dimension=0, tiled=True),
        lax.psum_scatter(total_gain_one, ("dp", "expert"), scatter_dimension=0, tiled=True),
        lax.psum_scatter(total_gain_two, ("dp", "expert"), scatter_dimension=0, tiled=True),
    )
    table_sum = lax.psum(total_table, ("dp", "expert"))
    grad_in_share, grad_out_share = (total_in, total_out)
    block_out = jnp.concatenate(out_blocks, axis=0)
    grad_tokens = jnp.concatenate(grad_blocks, axis=0)
    return (
        block_out,
        grad_tokens,
        dense_shares[0],
        dense_shares[1],
        dense_shares[2],
        dense_shares[3],
        dense_shares[4],
        dense_shares[5],
        dense_shares[6],
        table_sum,
        grad_in_share,
        grad_out_share,
    )


def solution(mesh):
    placed = (
        P(("dp", "expert"), None),
        P(("dp", "expert"), None),
        P(("dp", "expert"), None),
        P(("dp", "expert"), None),
        P(("dp", "expert"), None),
        P(("dp", "expert"), None),
        P(("dp", "expert"), None),
        P(("dp", "expert"), None),
        P(("dp", "expert"), None),
        P(("dp", "expert")),
        P(("dp", "expert")),
        P(),
        P("expert", None, "dp"),
        P("expert", "dp", None),
    )
    return jax.shard_map(
        local,
        mesh=mesh,
        in_specs=placed,
        out_specs=(
            P(("dp", "expert"), None),
            P(("dp", "expert"), None),
            P(("dp", "expert"), None),
            P(("dp", "expert"), None),
            P(("dp", "expert"), None),
            P(("dp", "expert"), None),
            P(("dp", "expert"), None),
            P(("dp", "expert")),
            P(("dp", "expert")),
            P(),
            P("expert", None, "dp"),
            P("expert", "dp", None),
        ),
        check_vma=False,
    )
```

profile of v0, /device:TPU:0, one launch (start us, length us, event | category | flops | bytes accessed | tf_op | source)
XLA Modules:
  0.0 1404.7 jit_solution(7090563331537020885)
XLA Ops:
  11.8 42.1 %all-reduce.6 = (bf16[768]{0:T(1024)(128)(2,1)S(1)}, bf16[768]{0:T(1024)(128)(2,1)S(1)}) all-reduce(bf16[768]{0:T(1024)(128)(2,1)S(1)} %dynamic-update-slice, bf16[768]{0:T(1024)(128)(2,1)S(1)} %dynamic-update-slice.1), channel_id=1, replica_groups=mesh['dp'=4,'expert'=8] {'dp','expert'}, use_global_device_ids=true, to_apply=%add | all-reduce | flops 1536 | bytes 6144
  57.2 10.7 fusion
  67.8 19.4 %copy.191 = f32[2,8,512,512]{3,2,1,0:T(8,128)} copy(f32[2,8,512,512]{3,1,2,0:T(8,128)S(1)} %bitcast.220) | data formatting | bytes 33554432
  87.2 10.7 slice.58
  97.9 12.7 copy.137
  112.3 40.7 %all-gather = bf16[32,24,16]{1,2,0:T(8,128)(2,1)S(1)} all-gather(bf16[1,24,16]{1,2,0:T(8,128)(2,1)S(1)} %bitcast.298), channel_id=1, replica_groups=mesh['dp'=4,'expert'=8] {'dp','expert'}, dimensions={0}, use_global_device_ids=true | all-gather | bytes 25344 | tf_op jit(solution)/shard_map/all_gather | solution.py:180
  166.3 14.2 %all-gather.10.cloned.1.call-done = bf16[768,768]{1,0:T(8,128)(2,1)} async-done(((bf16[24,768]{1,0:T(8,128)(2,1)}), bf16[768,768]{1,0:T(8,128)(2,1)}) %all-gather.10.cloned.1.call-update) | async-done | bytes 1179664 | tf_op jit(solution)/shard_map/all_gather | solution.py:178
  186.0 6.3 fusion.119
  199.1 37.3 %all-gather.16.cloned.1.call-done = bf16[768,768]{1,0:T(8,128)(2,1)} async-done(((bf16[24,768]{1,0:T(8,128)(2,1)}), bf16[768,768]{1,0:T(8,128)(2,1)}) %all-gather.16.cloned.1.call-update) | async-done | bytes 1179664 | tf_op jit(solution)/shard_map/all_gather | solution.py:179
  247.4 6.5 fusion.118
  262.3 6.9 fusion.56
  273.2 4.5 scatter_custom_fusion.2
  277.6 41.4 %all_to_all.132 = bf16[16,64,768]{2,1,0:T(8,128)(2,1)S(1)} all-to-all(bf16[16,64,768]{2,1,0:T(8,128)(2,1)} %bitcast.264), channel_id=1, replica_groups=mesh['dp'=4,'expert'=8] {'expert'}, dimensions={0} | all-to-all | bytes 3145728 | tf_op jit(solution)/shard_map/all_to_all | solution.py:303
  320.5 4.0 scatter_custom_fusion
  324.5 41.4 %all_to_all.133 = bf16[16,64,768]{2,1,0:T(8,128)(2,1)S(1)} all-to-all(bf16[16,64,768]{2,1,0:T(8,128)(2,1)} %bitcast.265), channel_id=1, replica_groups=mesh['dp'=4,'expert'=8] {'expert'}, dimensions={0} | all-to-all | bytes 3145728 | tf_op jit(solution)/shard_map/all_to_all | solution.py:221
  369.3 4.5 scatter_custom_fusion.3
  373.7 41.3 %all_to_all.134 = bf16[16,64,768]{2,1,0:T(8,128)(2,1)S(1)} all-to-all(bf16[16,64,768]{2,1,0:T(8,128)(2,1)} %bitcast.266), channel_id=1, replica_groups=mesh['dp'=4,'expert'=8] {'expert'}, dimensions={0} | all-to-all | bytes 3145728 | tf_op jit(solution)/shard_map/all_to_all | solution.py:303
  420.2 41.3 %all_to_all.135 = bf16[16,64,768]{2,1,0:T(8,128)(2,1)S(1)} all-to-all(bf16[16,64,768]{2,1,0:T(8,128)(2,1)} %bitcast.267), channel_id=1, replica_groups=mesh['dp'=4,'expert'=8] {'expert'}, dimensions={0} | all-to-all | bytes 3145728 | tf_op jit(solution)/shard_map/all_to_all | solution.py:221
  462.9 11.4 fusion.122
  474.3 19.7 %fusion.12 = (bf16[2,2048,768]{2,1,0:T(8,128)(2,1)}, f32[2,2048,768]{2,1,0:T(8,128)}) fusion(f32[2,2048,768]{2,1,0:T(8,128)} %fusion.122, bf16[2,2048,768]{2,1,0:T(8,128)(2,1)} %all-gather.18.cloned.1.call-done, bf16[2,768,768]{2,1,0:T(8,128)(2,1)S(1)} %copy-done), kind=kOutput, calls=%fused_computation.26 | convolution fusion | flops 4894752768 | bytes 40108032 | tf_op jit(solution)/shard_map/erd,edf->erf/dot_general | solution.py:229
  493.9 12.2 convolution_convert_fusion.3
  506.1 27.0 %all-gather.24.cloned.1.call-done = bf16[2,2048,768]{2,1,0:T(8,128)(2,1)} async-done(((bf16[2,512,768]{2,1,0:T(8,128)(2,1)}), bf16[2,2048,768]{2,1,0:T(8,128)(2,1)}) %all-gather.24.cloned.1.call-update) | async-done | bytes 6291472 | tf_op jit(solution)/shard_map/all_gather | solution.py:310
  533.1 10.9 fusion.125
  544.1 61.7 %all-gather.20.cloned.1.call-done = bf16[2,2048,768]{2,1,0:T(8,128)(2,1)} async-done(((bf16[2,512,768]{2,1,0:T(8,128)(2,1)}), bf16[2,2048,768]{2,1,0:T(8,128)(2,1)}) %all-gather.20.cloned.1.call-update) | async-done | bytes 6291472 | tf_op jit(solution)/shard_map/all_gather | solution.py:228
  605.8 19.8 %fusion.19 = (bf16[2,2048,768]{2,1,0:T(8,128)(2,1)}, f32[2,2048,768]{2,1,0:T(8,128)}) fusion(f32[2,2048,768]{2,1,0:T(8,128)} %fusion.125, bf16[2,2048,768]{2,1,0:T(8,128)(2,1)} %all-gather.20.cloned.1.call-done, bf16[2,768,768]{2,1,0:T(8,128)(2,1)S(1)} %copy-done), kind=kOutput, calls=%fused_computation.33 | convolution fusion | flops 4894752768 | bytes 40108032 | tf_op jit(solution)/shard_map/erd,edf->erf/dot_general | solution.py:229
  625.6 12.5 convolution_convert_fusion.2
  638.2 9.8 convolution_convert_fusion
  648.1 10.0 convolution_convert_fusion.1
  658.2 20.8 %reduce-scatter.10.cloned.1.call-done = bf16[2,512,768]{2,1,0:T(8,128)(2,1)} async-done(((bf16[2,2048,768]{2,1,0:T(8,128)(2,1)}), bf16[2,512,768]{2,1,0:T(8,128)(2,1)}) %reduce-scatter.10.cloned.1.call-update) | async-done | bytes 1572880 | tf_op jit(solution)/shard_map/reduce_scatter | solution.py:236
  679.0 4.2 copy.142
  683.2 4.6 all-to-all-start.1
  687.8 64.3 %reduce-scatter.12.cloned.1.call-done = bf16[2,512,768]{2,1,0:T(8,128)(2,1)} async-done(((bf16[2,2048,768]{2,1,0:T(8,128)(2,1)}), bf16[2,512,768]{2,1,0:T(8,128)(2,1)}) %reduce-scatter.12.cloned.1.call-update) | async-done | bytes 1572880 | tf_op jit(solution)/shard_map/reduce_scatter | solution.py:236
  752.0 4.2 copy.151
  757.4 4.6 all-to-all-start.3
  762.0 63.2 %reduce-scatter.16.cloned.1.call-done = bf16[2,512,768]{2,1,0:T(8,128)(2,1)} async-done(((bf16[2,2048,768]{2,1,0:T(8,128)(2,1)}), bf16[2,512,768]{2,1,0:T(8,128)(2,1)}) %reduce-scatter.16.cloned.1.call-update) | async-done | bytes 1572880 | tf_op jit(solution)/shard_map/reduce_scatter | solution.py:325
  825.3 4.2 copy.161
  829.4 4.6 all-to-all-start.7
  834.1 13.6 fusion.116
  847.7 50.6 %reduce-scatter.14.cloned.1.call-done = bf16[2,512,768]{2,1,0:T(8,128)(2,1)} async-done(((bf16[2,2048,768]{2,1,0:T(8,128)(2,1)}), bf16[2,512,768]{2,1,0:T(8,128)(2,1)}) %reduce-scatter.14.cloned.1.call-update) | async-done | bytes 1572880 | tf_op jit(solution)/shard_map/reduce_scatter | solution.py:325
  898.3 4.2 copy.154
  903.7 4.6 all-to-all-start.5
  908.4 10.9 fusion.128
  919.3 13.7 convolution_add_fusion
  938.1 4.1 gather_fusion.1
  967.7 7.5 fusion.65
  975.2 7.6 fusion.59
  990.2 6.7 multiply_reduce_fusion
  996.9 7.1 multiply_convert_fusion
  1012.0 10.6 multiply_reduce_fusion.1
  1023.6 6.9 multiply_convert_fusion.1
  1036.6 11.7 convolution_add_fusion.1
  1048.5 4.1 multiply_convert_fusion.5
  1068.0 8.8 copy.167
  1076.8 8.7 copy.168
  1085.5 6.8 pad.8
  1092.3 11.4 copy.192
  1103.7 6.9 pad.9
  1110.6 11.7 copy.193
  1122.3 7.3 fusion.1
  1129.7 4.5 fusion.68
  1134.2 40.8 %all-reduce.5 = (f32[768,16]{0,1:T(8,128)S(1)}, f32[768]{0:T(1024)S(1)}, f32[768]{0:T(1024)S(1)}, f32[32,12]{0,1:T(8,128)}) all-reduce(f32[768,16]{0,1:T(8,128)S(1)} %convolution_add_fusion.6, f32[768]{0:T(1024)S(1)} %add.353, f32[768]{0:T(1024)S(1)} %add.354, ...), channel_id=10, replica_groups=mesh['dp'=4,'expert'=8] {'dp','expert'}, use_global_device_ids=true, to_apply=%region_44.45.clone | all-reduce | flops 14208 | bytes 113664
  1183.7 5.8 reduce-scatter.22.cloned.1.call-done
  1189.5 103.7 %reduce-scatter.20.cloned.1.call-done = f32[24,768]{1,0:T(8,128)} async-done(((f32[768,768]{1,0:T(8,128)}), f32[24,768]{1,0:T(8,128)}) %reduce-scatter.20.cloned.1.call-update) | async-done | bytes 73744 | tf_op jit(solution)/shard_map/reduce_scatter | solution.py:373
  1293.3 104.6 %reduce-scatter.18.cloned.1.call-done = f32[24,768]{1,0:T(8,128)} async-done(((f32[768,768]{1,0:T(8,128)}), f32[24,768]{1,0:T(8,128)}) %reduce-scatter.18.cloned.1.call-update) | async-done | bytes 73744 | tf_op jit(solution)/shard_map/reduce_scatter | solution.py:372
  (413 shorter events, 148.5 us)
Async XLA Ops:
  7.2 467.1 %copy-start = (bf16[2,768,768]{2,1,0:T(8,128)(2,1)S(1)}, bf16[2,768,768]{2,1,0:T(8,128)(2,1)}, u32[]{:S(2)}) copy-start(bf16[2,768,768]{2,1,0:T(8,128)(2,1)} %param.26) | copy-start | bytes 7077892
  7.2 150.9 %all-gather.12.cloned.1.call-start = ((), (), s32[]{:S(2)}) async-start(), calls=%async_computation.17 | async-start | bytes 1216512 | tf_op jit(solution)/shard_map/all_gather | solution.py:176
  7.9 153.7 %all-gather.14.cloned.1.call-start = ((), (), s32[]{:S(2)}) async-start(), calls=%async_computation.18 | async-start | bytes 1216512 | tf_op jit(solution)/shard_map/all_gather | solution.py:177
  8.7 171.7 %all-gather.10.cloned.1.call-start = ((), (), s32[]{:S(2)}) async-start(), calls=%async_computation.16 | async-start | bytes 1216512 | tf_op jit(solution)/shard_map/all_gather | solution.py:178
  9.4 227.0 %all-gather.16.cloned.1.call-start = ((), (), s32[]{:S(2)}) async-start(), calls=%async_computation.19 | async-start | bytes 1216512 | tf_op jit(solution)/shard_map/all_gather | solution.py:179
  10.0 452.9 %all-gather.22.cloned.1.call-start = ((), (), s32[]{:S(2)}) async-start(), calls=%async_computation.24 | async-start | bytes 7864320 | tf_op jit(solution)/shard_map/all_gather | solution.py:310
  53.9 205.2 %copy-start.70 = (f32[768]{0:T(1024)}, f32[768]{0:T(1024)S(1)}, u32[]{:S(2)}) copy-start(f32[768]{0:T(1024)S(1)} %convert_element_type.320) | copy-start | bytes 9220
  57.1 10.7 copy-start.45
  97.9 12.7 copy-start.107
  97.9 14.4 %copy-start.106 = (bf16[24,16]{0,1:T(8,128)(2,1)S(1)}, bf16[24,16]{0,1:T(8,128)(2,1)}, u32[]{:S(2)}) copy-start(bf16[24,16]{0,1:T(8,128)(2,1)} %param.22) | copy-start | bytes 2308
  97.9 55.3 %copy-start.98 = (s32[1024,1]{0,1:T(1,128)S(1)}, s32[1024,1]{0,1:T(1,128)}, u32[]{:S(2)}) copy-start(s32[1024,1]{0,1:T(1,128)} %param.17) | copy-start | bytes 12292
  112.3 158.6 %copy-start.76 = (f32[768]{0:T(1024)}, f32[768]{0:T(1024)S(1)}, u32[]{:S(2)}) copy-start(f32[768]{0:T(1024)S(1)} %convert_element_type.337) | copy-start | bytes 9220
  153.3 213.9 %copy-start.68 = (bf16[768,16]{0,1:T(8,128)(2,1)}, bf16[768,16]{0,1:T(8,128)(2,1)S(1)}, u32[]{:S(2)}) copy-start(bf16[768,16]{0,1:T(8,128)(2,1)S(1)} %reshape.517) | copy-start | bytes 73732
  153.3 119.3 %copy-start.72 = (s32[512,1]{0,1:T(1,128)}, s32[512,1]{0,1:T(1,128)S(1)}, u32[]{:S(2)}) copy-start(s32[512,1]{0,1:T(1,128)S(1)} %get-tuple-element.44) | copy-start | bytes 6148
  153.3 215.3 %copy-start.74 = (s32[512,1]{0,1:T(1,128)}, s32[512,1]{0,1:T(1,128)S(1)}, u32[]{:S(2)}) copy-start(s32[512,1]{0,1:T(1,128)S(1)} %get-tuple-element.45) | copy-start | bytes 6148
  157.5 22.9 %copy-start.84 = (f32[512]{0:T(512)}, f32[512]{0:T(512)S(1)}, u32[]{:S(2)}) copy-start(f32[512]{0:T(512)S(1)} %get-tuple-element.49) | copy-start | bytes 6148
  157.5 101.6 %copy-start.78 = (f32[512]{0:T(512)}, f32[512]{0:T(512)S(1)}, u32[]{:S(2)}) copy-start(f32[512]{0:T(512)S(1)} %get-tuple-element.78) | copy-start | bytes 6148
  166.3 19.7 %copy-start.20 = (bf16[512,768]{0,1:T(8,128)(2,1)}, bf16[512,768]{0,1:T(8,128)(2,1)S(1)}, u32[]{:S(2)}) copy-start(bf16[512,768]{0,1:T(8,128)(2,1)S(1)} %copy.146) | copy-start | bytes 2359300
  199.1 41.0 %copy-start.48 = (bf16[12,64,512]{2,1,0:T(8,128)(2,1)}, bf16[12,64,512]{2,1,0:T(8,128)(2,1)S(1)}, u32[]{:S(2)}) copy-start(bf16[12,64,512]{2,1,0:T(8,128)(2,1)S(1)} %fusion.62) | copy-start | bytes 2359300
  247.4 6.5 copy-start.22
  262.3 7.0 copy-start.27
  262.3 7.0 copy-start.8
  262.3 7.0 copy-start.113
  272.2 48.3 %copy-start.34 = (bf16[512,768]{1,0:T(8,128)(2,1)}, bf16[512,768]{1,0:T(8,128)(2,1)S(1)}, u32[]{:S(2)}) copy-start(bf16[512,768]{1,0:T(8,128)(2,1)S(1)} %get-tuple-element.40) | copy-start | bytes 2359300
  272.5 46.5 %copy-start.80 = (f32[512]{0:T(512)}, f32[512]{0:T(512)S(1)}, u32[]{:S(2)}) copy-start(f32[512]{0:T(512)S(1)} %get-tuple-element.64) | copy-start | bytes 6148
  273.1 45.9 %copy-start.90 = (f32[512]{0:T(512)}, f32[512]{0:T(512)S(1)}, u32[]{:S(2)}) copy-start(f32[512]{0:T(512)S(1)} %fusion.97) | copy-start | bytes 6148
  273.1 45.9 %copy-start.94 = (f32[512]{0:T(512)}, f32[512]{0:T(512)S(1)}, u32[]{:S(2)}) copy-start(f32[512]{0:T(512)S(1)} %multiply_reduce_fusion.9) | copy-start | bytes 6148
  320.4 153.9 %all-gather.18.cloned.1.call-start = ((), (), s32[]{:S(2)}) async-start(), calls=%async_computation.20 | async-start | bytes 7864320 | tf_op jit(solution)/shard_map/all_gather | solution.py:228
  367.2 166.0 %all-gather.24.cloned.1.call-start = ((), (), s32[]{:S(2)}) async-start(), calls=%async_computation.26 | async-start | bytes 7864320 | tf_op jit(solution)/shard_map/all_gather | solution.py:310
  368.6 46.5 %copy-start.82 = (f32[512]{0:T(512)}, f32[512]{0:T(512)S(1)}, u32[]{:S(2)}) copy-start(f32[512]{0:T(512)S(1)} %get-tuple-element.68) | copy-start | bytes 6148
  369.2 45.9 %copy-start.92 = (f32[512]{0:T(512)}, f32[512]{0:T(512)S(1)}, u32[]{:S(2)}) copy-start(f32[512]{0:T(512)S(1)} %fusion.99) | copy-start | bytes 6148
  369.2 45.8 %copy-start.96 = (f32[512]{0:T(512)}, f32[512]{0:T(512)S(1)}, u32[]{:S(2)}) copy-start(f32[512]{0:T(512)S(1)} %multiply_reduce_fusion.8) | copy-start | bytes 6148
  416.4 189.4 %all-gather.20.cloned.1.call-start = ((), (), s32[]{:S(2)}) async-start(), calls=%async_computation.22 | async-start | bytes 7864320 | tf_op jit(solution)/shard_map/all_gather | solution.py:228
  462.8 216.2 %reduce-scatter.10.cloned.1.call-start = ((), (), s32[]{:S(2)}) async-start(), calls=%async_computation.21 | async-start | bytes 7864320 | tf_op jit(solution)/shard_map/reduce_scatter | solution.py:236
  474.3 19.7 %copy-start.108 = (bf16[2,768,768]{2,1,0:T(8,128)(2,1)S(1)}, bf16[2,768,768]{2,1,0:T(8,128)(2,1)}, u32[]{:S(2)}) copy-start(bf16[2,768,768]{2,1,0:T(8,128)(2,1)} %param.27) | copy-start | bytes 7077892
  506.1 245.9 %reduce-scatter.12.cloned.1.call-start = ((), (), s32[]{:S(2)}) async-start(), calls=%async_computation.23 | async-start | bytes 7864320 | tf_op jit(solution)/shard_map/reduce_scatter | solution.py:236
  605.8 19.8 %copy-start.109 = (bf16[2,768,768]{2,1,0:T(8,128)(2,1)S(1)}, bf16[2,768,768]{2,1,0:T(8,128)(2,1)}, u32[]{:S(2)}) copy-start(bf16[2,768,768]{2,1,0:T(8,128)(2,1)} %param.27) | copy-start | bytes 7077892
  638.2 187.1 %reduce-scatter.16.cloned.1.call-start = ((), (), s32[]{:S(2)}) async-start(), calls=%async_computation.27 | async-start | bytes 7864320 | tf_op jit(solution)/shard_map/reduce_scatter | solution.py:325
  648.1 250.3 %reduce-scatter.14.cloned.1.call-start = ((), (), s32[]{:S(2)}) async-start(), calls=%async_computation.25 | async-start | bytes 7864320 | tf_op jit(solution)/shard_map/reduce_scatter | solution.py:325
  683.2 73.1 %all-to-all-start.1 = ((bf16[2,512,768]{2,0,1:T(2,128)(2,1)}), bf16[2,512,768]{2,0,1:T(2,128)(2,1)S(1)}, u32[]{:S(2)}, u32[]{:S(2)}) async-start(bf16[2,512,768]{2,0,1:T(2,128)(2,1)} %copy.142), calls=%async_computation.2 | async-start | bytes 3145728 | tf_op jit(solution)/shard_map/all_to_all | solution.py:239
  757.4 72.0 %all-to-all-start.3 = ((bf16[2,512,768]{2,0,1:T(2,128)(2,1)}), bf16[2,512,768]{2,0,1:T(2,128)(2,1)}, u32[]{:S(2)}, u32[]{:S(2)}) async-start(bf16[2,512,768]{2,0,1:T(2,128)(2,1)} %copy.151), calls=%async_computation.5 | async-start | bytes 3145728 | tf_op jit(solution)/shard_map/all_to_all | solution.py:239
  829.4 73.0 %all-to-all-start.7 = ((bf16[2,512,768]{2,0,1:T(2,128)(2,1)}), bf16[2,512,768]{2,0,1:T(2,128)(2,1)S(1)}, u32[]{:S(2)}, u32[]{:S(2)}) async-start(bf16[2,512,768]{2,0,1:T(2,128)(2,1)} %copy.161), calls=%async_computation.11 | async-start | bytes 3145728 | tf_op jit(solution)/shard_map/all_to_all | solution.py:328
  903.7 42.9 %all-to-all-start.5 = ((bf16[2,512,768]{2,0,1:T(2,128)(2,1)}), bf16[2,512,768]{2,0,1:T(2,128)(2,1)}, u32[]{:S(2)}, u32[]{:S(2)}) async-start(bf16[2,512,768]{2,0,1:T(2,128)(2,1)} %copy.154), calls=%async_computation.8 | async-start | bytes 3145728 | tf_op jit(solution)/shard_map/all_to_all | solution.py:328
  908.3 275.4 %reduce-scatter.24.cloned.1.call-start = ((), (), s32[]{:S(2)}) async-start(), calls=%async_computation.31 | async-start | bytes 2433024 | tf_op jit(solution)/shard_map/reduce_scatter | solution.py:375
  919.3 13.7 copy-start.41
  961.9 5.8 copy-start.29
  967.7 7.5 copy-start.67
  975.2 7.7 copy-start.24
  975.2 7.7 copy-start.51
  985.1 204.5 %reduce-scatter.22.cloned.1.call-start = ((), (), s32[]{:S(2)}) async-start(), calls=%async_computation.30 | async-start | bytes 2433024 | tf_op jit(solution)/shard_map/reduce_scatter | solution.py:374
  996.9 9.8 copy-start.30
  1009.6 283.6 %reduce-scatter.20.cloned.1.call-start = ((), (), s32[]{:S(2)}) async-start(), calls=%async_computation.29 | async-start | bytes 2433024 | tf_op jit(solution)/shard_map/reduce_scatter | solution.py:373
  1009.7 12.9 slice-start
  1012.0 10.6 slice-start.1
  1012.0 11.6 slice-start.2
  1023.6 6.9 copy-start.31
  1036.5 11.7 copy-start.37
  1036.5 361.4 %reduce-scatter.18.cloned.1.call-start = ((), (), s32[]{:S(2)}) async-start(), calls=%async_computation.28 | async-start | bytes 2433024 | tf_op jit(solution)/shard_map/reduce_scatter | solution.py:372
  1036.6 11.9 copy-start.21
  1110.6 19.1 %slice-start.5 = ((s8[8388608]{0:T(1024)(128)(4,1)}), s8[4194304]{0:T(1024)(128)(4,1)S(1)}, s32[]{:S(2)}) async-start(s8[8388608]{0:T(1024)(128)(4,1)} %bitcast.232), calls=%async_computation.37 | async-start | bytes 8388608
  1122.3 7.4 slice-start.6
  1122.3 7.4 copy-start.46
  1129.7 47.2 %copy-start.52 = (bf16[512,768]{1,0:T(8,128)(2,1)S(1)}, bf16[512,768]{1,0:T(8,128)(2,1)}, u32[]{:S(2)}) copy-start(bf16[512,768]{1,0:T(8,128)(2,1)} %get-tuple-element.36) | copy-start | bytes 2359300
  1181.9 216.1 %copy-start.1 = (bf16[2,768,768]{2,1,0:T(8,128)(2,1)S(1)}, bf16[2,768,768]{2,1,0:T(8,128)(2,1)}, u32[]{:S(2)}) copy-start(bf16[2,768,768]{2,1,0:T(8,128)(2,1)} %param.26) | copy-start | bytes 7077892
  (80 other events, 188.9 us)
Sparse Core Ops, SparseCore 0:
  11.1 56.9 all-gather.11
  71.1 53.1 all-gather.13
  127.4 53.0 all-gather.9
  183.3 53.1 all-gather.15
  320.5 68.0 all-gather.21
  390.3 70.1 all-gather.17
  463.0 70.1 all-gather.23
  535.6 70.1 all-gather.19
  608.7 70.2 reduce-scatter.9
  681.8 70.1 reduce-scatter.11
  755.0 70.1 reduce-scatter.15
  828.1 70.1 reduce-scatter.13
  985.2 99.4 reduce-scatter.23
  1091.3 98.1 reduce-scatter.21
  1195.2 97.9 reduce-scatter.19
  1299.8 98.0 reduce-scatter.17
where the time goes:
time: 1410 us; the launch traced here: 1400 us
  waiting for transfers between devices  556 us (39%)
  matrix products  295 us (21%)
  blocking collectives  289 us (20%)
  local copies, waits for them, and re-layouts  180 us (13%)
  other arithmetic  49 us (3%)
  starting transfers between devices  19.1 us (1%)
  between operations  15.7 us (1%)
    all_to_all x4, blocking collectives, local(): lax.all_to_all(buffer.reshape(expert_total, capacity, model_width), 'expe...  165 us
    reduce_scatter x2, waiting for transfers between devices, local(): lax.psum_scatter(partial_back.astype(jnp.bfloat16), 'dp', scatter_dimensi...  114 us
    reduce_scatter x1, waiting for transfers between devices, local(): lax.psum_scatter(total_query, ('dp', 'expert'), scatter_dimension=0, tile...  105 us
    reduce_scatter x1, waiting for transfers between devices, local(): lax.psum_scatter(total_key, ('dp', 'expert'), scatter_dimension=0, tiled=...  104 us
    reduce_scatter x2, waiting for transfers between devices, local(): lax.psum_scatter(partial_value.astype(jnp.bfloat16), 'dp', scatter_dimens...  85.1 us
    unnamed x2, blocking collectives  82.9 us
    unnamed x263, local copies, waits for them, and re-layouts  82 us
    all_gather x2, waiting for transfers between devices, local(): expert_rows = lax.all_gather(received, 'dp', axis=1, tiled=True)  61.7 us
  transfers between devices with their start and end apart: 20, of which 11 were waited for; matrix products, arithmetic and copies ran while one was open for 30% of the time, Pallas kernels for 0%

commit v1 on v0

v1 whole, which is shorter than its diff:
```python
import jax
import jax.numpy as jnp
from jax import lax
from jax.sharding import PartitionSpec as P

H = 12
HD = 64


EPSILON = 1e-06
THRESHOLDS = (12, 16, 23, 32, 46, 64, 91)
NEGATIVE = -1e30


def bucket_grid(extent):
    places = jnp.arange(extent, dtype=jnp.int32)
    offset = places[None, :] - places[:, None]
    spread = jnp.abs(offset)
    beyond = 8 + sum(((spread >= threshold).astype(jnp.int32) for threshold in THRESHOLDS))
    return jnp.where(offset > 0, 16, 0).astype(jnp.int32) + jnp.where(spread < 8, spread, beyond)


def same_sequence(seq_lengths, extent):
    places = jnp.arange(extent, dtype=jnp.int32)
    ending = jnp.cumsum(seq_lengths)
    segment = jnp.sum((places[:, None] >= ending[None, :]).astype(jnp.int32), axis=1)
    return segment[:, None] == segment[None, :]


def gelu_tanh(values):
    return jax.nn.gelu(values, approximate=True)


def rms_forward(values, gain_vector):
    scale_row = lax.rsqrt(jnp.mean(values * values, axis=-1, keepdims=True) + EPSILON)
    return (scale_row, values * scale_row * gain_vector)


def rms_backward(values, scale_row, gain_vector, grad_scaled):
    weighted = grad_scaled * gain_vector
    grad_values = scale_row * weighted - values * scale_row**3 * jnp.mean(
        weighted * values, axis=-1, keepdims=True
    )
    grad_gain = jnp.sum(grad_scaled * values * scale_row, axis=0)
    return (grad_values, grad_gain)


def contract_rows(former, latter):
    return lax.dot_general(
        former, latter, (((0,), (0,)), ((), ())), preferred_element_type=jnp.float32
    )


def contract_cols(former, latter):
    return lax.dot_general(
        former, latter, (((1,), (1,)), ((), ())), preferred_element_type=jnp.float32
    )


def attention_scores(query, key, bias_grid, allowed):
    scores = jnp.einsum("bphd,bqhd->bhpq", query, key, preferred_element_type=jnp.float32)
    return jnp.where(allowed[:, None], scores * HD ** (-0.5) + bias_grid[None], NEGATIVE)


def sum_everywhere(values, axes):
    count = lax.axis_size(axes)
    step = 1
    while step < count:
        values = values + lax.ppermute(values, axes, [(i, i ^ step) for i in range(count)])
        step *= 2
    return values


def sum_scatter(values):
    part = lax.psum_scatter(values, "dp", scatter_dimension=0, tiled=True)
    return lax.psum_scatter(part, "expert", scatter_dimension=0, tiled=True)


def lane_padded(parts):
    joined = jnp.concatenate(parts, axis=1)
    return jnp.pad(joined, ((0, 0), (0, -joined.shape[1] % 128)))


def local(
    tokens,
    cotangent,
    lengths,
    routes,
    w_query,
    w_key,
    w_value,
    w_output,
    router,
    gain_first,
    gain_second,
    bias_table,
    w_in,
    w_out,
):
    f32, bf16 = jnp.float32, jnp.bfloat16
    blocks = lengths.shape[0]
    rows, width = tokens.shape
    extent = rows // blocks
    expert_local = w_in.shape[0]
    lanes = lax.axis_size("expert")
    groups = lax.axis_size("dp")
    expert_total = expert_local * lanes
    capacity = 2 * extent // expert_total
    bucket_count = bias_table.shape[0]

    packed = lane_padded(
        (w_query, w_key, w_value, w_output, router, gain_first[:, None], gain_second[:, None])
    )
    dense = lax.all_gather(packed, "expert", axis=0, tiled=True)
    dense = lax.all_gather(dense, "dp", axis=0, tiled=True)
    dense, w_in, w_out = lax.optimization_barrier((dense, w_in, w_out))
    w_in_all = lax.all_gather(w_in, "dp", axis=0, tiled=False)
    w_out_all = lax.all_gather(w_out, "dp", axis=0, tiled=False)
    weight_qkv = dense[:, : 3 * width]
    weight_output = dense[:, 3 * width : 4 * width]
    router_full = dense[:, 4 * width : 4 * width + expert_total]
    gain_one = dense[:, 4 * width + expert_total].astype(f32)
    gain_two = dense[:, 4 * width + expert_total + 1].astype(f32)

    bucket_flat = bucket_grid(extent).reshape(1, extent * extent)
    bucket_hot = (jnp.arange(bucket_count, dtype=jnp.int32)[:, None] == bucket_flat)
    bias_grid = lax.dot_general(
        bias_table,
        bucket_hot.astype(f32),
        (((0,), (0,)), ((), ())),
        precision=lax.Precision.HIGHEST,
        preferred_element_type=f32,
    ).reshape(H, extent, extent)
    allowed = jax.vmap(lambda own: same_sequence(own, extent))(lengths)

    rows_in = tokens.astype(f32)
    scale_one, scaled_one = rms_forward(rows_in, gain_one)
    normed = scaled_one.astype(bf16)
    qkv = jnp.dot(normed, weight_qkv, preferred_element_type=f32).astype(bf16)
    shape = (blocks, extent, H, HD)
    query = qkv[:, :width].reshape(shape)
    key = qkv[:, width : 2 * width].reshape(shape)
    value = qkv[:, 2 * width :].reshape(shape)
    masked = attention_scores(query, key, bias_grid, allowed)
    row_peak = jnp.max(masked, axis=-1, keepdims=True)
    log_total = row_peak + jnp.log(jnp.sum(jnp.exp(masked - row_peak), axis=-1, keepdims=True))
    soft_low = jnp.exp(masked - log_total).astype(bf16)
    context = jnp.einsum("bhpq,bqhd->bphd", soft_low, value, preferred_element_type=f32)
    context = context.reshape(rows, width).astype(bf16)

    middle = rows_in + jnp.dot(context, weight_output, preferred_element_type=f32)
    scale_two, scaled_two = rms_forward(middle, gain_two)
    second = scaled_two.astype(bf16)
    logits = jnp.dot(second, router_full, preferred_element_type=f32)
    exps = jnp.exp(logits - jnp.max(logits, axis=-1, keepdims=True))
    gate_probs = exps / jnp.sum(exps, axis=-1, keepdims=True)
    choose = (routes == jnp.arange(expert_total, dtype=jnp.int32)[None, :]).astype(jnp.int32)
    by_block = choose.reshape(blocks, extent, expert_total)
    slot = jnp.sum(jnp.cumsum(by_block, axis=1) * by_block, axis=-1) - 1
    place = (
        routes[:, 0].reshape(blocks, extent) * (blocks * capacity)
        + jnp.arange(blocks, dtype=jnp.int32)[:, None] * capacity
        + slot
    ).reshape(rows)
    choose_float = choose.astype(f32)
    gate = jnp.sum(gate_probs * choose_float, axis=-1, keepdims=True)
    final = cotangent.astype(f32)
    grad_expert = (gate * final).astype(bf16)

    share = expert_local * blocks * capacity

    def dispatch(values):
        buffer = jnp.zeros((expert_total * blocks * capacity, width), bf16).at[place].set(values)
        got = lax.all_to_all(
            buffer.reshape(lanes, share, width), "expert", split_axis=0, concat_axis=0, tiled=True
        )
        got = got.reshape(lanes, expert_local, blocks * capacity, width)
        return got.transpose(1, 0, 2, 3).reshape(expert_local, lanes * blocks * capacity, width)

    def collect(values):
        sent = values.reshape(expert_local, lanes, blocks * capacity, width).transpose(1, 0, 2, 3)
        got = lax.all_to_all(
            sent.reshape(lanes, share, width), "expert", split_axis=0, concat_axis=0, tiled=True
        )
        return got.reshape(expert_total * blocks * capacity, width)[place].astype(f32)

    expert_rows = dispatch(second)
    grad_rows = dispatch(grad_expert)

    out_total = 0.0
    back_total = 0.0
    hiddens = []
    grad_pres = []
    for group in range(groups):
        pre = jnp.einsum("erd,edf->erf", expert_rows, w_in_all[group], preferred_element_type=f32)
        grad_hidden = jnp.einsum(
            "erd,efd->erf", grad_rows, w_out_all[group], preferred_element_type=f32
        )
        activated, pull = jax.vjp(gelu_tanh, pre)
        hidden = activated.astype(bf16)
        grad_pre = pull(grad_hidden)[0].astype(bf16)
        out_total = out_total + jnp.einsum(
            "erf,efd->erd", hidden, w_out_all[group], preferred_element_type=f32
        )
        back_total = back_total + jnp.einsum(
            "erf,edf->erd", grad_pre, w_in_all[group], preferred_element_type=f32
        )
        hiddens.append(hidden)
        grad_pres.append(grad_pre)
    expert_out = collect(out_total.astype(bf16))
    grad_second = collect(back_total.astype(bf16))
    grad_in_parts = jnp.stack(
        [
            jnp.einsum("erd,erf->edf", expert_rows, own, preferred_element_type=f32).astype(bf16)
            for own in grad_pres
        ]
    )
    grad_in = lax.psum_scatter(grad_in_parts, "dp", scatter_dimension=0, tiled=True)
    grad_out_parts = jnp.stack(
        [
            jnp.einsum("erf,erd->efd", own, grad_rows, preferred_element_type=f32).astype(bf16)
            for own in hiddens
        ]
    )
    grad_out = lax.psum_scatter(grad_out_parts, "dp", scatter_dimension=0, tiled=True)

    block_out = (middle + gate * expert_out).astype(bf16)
    grad_gate = jnp.sum(final * expert_out, axis=-1, keepdims=True)
    grad_logits = (gate_probs * (choose_float * grad_gate - gate * grad_gate)).astype(bf16)
    grad_router = contract_rows(second, grad_logits)
    grad_second = grad_second + contract_cols(grad_logits, router_full)
    grad_part, grad_gain_two = rms_backward(middle, scale_two, gain_two, grad_second)
    grad_middle = final + grad_part
    grad_attended = grad_middle.astype(bf16)
    early = lane_padded(
        (contract_rows(context, grad_attended), grad_router, grad_gain_two[:, None])
    ).astype(bf16)
    early = sum_scatter(early).astype(f32)
    grad_context = contract_cols(grad_attended, weight_output).astype(bf16).reshape(shape)

    soft = jnp.exp(attention_scores(query, key, bias_grid, allowed) - log_total)
    grad_soft = jnp.einsum("bphd,bqhd->bhpq", grad_context, value, preferred_element_type=f32)
    grad_value = jnp.einsum(
        "bhpq,bphd->bqhd", soft.astype(bf16), grad_context, preferred_element_type=f32
    )
    inner = jnp.sum(grad_soft * soft, axis=-1, keepdims=True)
    grad_scores = (soft * (grad_soft - inner)).astype(bf16)
    grad_query = jnp.einsum("bhpq,bqhd->bphd", grad_scores, key, preferred_element_type=f32)
    grad_key = jnp.einsum("bhpq,bphd->bqhd", grad_scores, query, preferred_element_type=f32)
    grad_qkv = jnp.concatenate(
        [
            (grad_query * HD ** (-0.5)).astype(bf16).reshape(rows, width),
            (grad_key * HD ** (-0.5)).astype(bf16).reshape(rows, width),
            grad_value.astype(bf16).reshape(rows, width),
        ],
        axis=1,
    )
    table_rows = jnp.sum(grad_scores.astype(f32), axis=0).astype(bf16)
    grad_table = lax.dot_general(
        bucket_hot.astype(bf16),
        table_rows.reshape(H, extent * extent),
        (((1,), (1,)), ((), ())),
        preferred_element_type=f32,
    )
    grad_table = sum_everywhere(grad_table, ("dp", "expert"))
    grad_normed = contract_cols(grad_qkv, weight_qkv)
    grad_part, grad_gain_one = rms_backward(rows_in, scale_one, gain_one, grad_normed)
    grad_tokens = grad_middle + grad_part
    late = lane_padded((contract_rows(normed, grad_qkv), grad_gain_one[:, None])).astype(bf16)
    late = sum_scatter(late).astype(f32)
    return (
        block_out,
        grad_tokens,
        late[:, :width],
        late[:, width : 2 * width],
        late[:, 2 * width : 3 * width],
        early[:, :width],
        early[:, width : width + expert_total],
        late[:, 3 * width],
        early[:, width + expert_total],
        grad_table,
        grad_in.astype(f32).reshape(w_in.shape),
        grad_out.astype(f32).reshape(w_out.shape),
    )


def solution(mesh):
    placed = (
        P(("dp", "expert"), None),
        P(("dp", "expert"), None),
        P(("dp", "expert"), None),
        P(("dp", "expert"), None),
        P(("dp", "expert"), None),
        P(("dp", "expert"), None),
        P(("dp", "expert"), None),
        P(("dp", "expert"), None),
        P(("dp", "expert"), None),
        P(("dp", "expert")),
        P(("dp", "expert")),
        P(),
        P("expert", None, "dp"),
        P("expert", "dp", None),
    )
    return jax.shard_map(
        local,
        mesh=mesh,
        in_specs=placed,
        out_specs=(
            P(("dp", "expert"), None),
            P(("dp", "expert"), None),
            P(("dp", "expert"), None),
            P(("dp", "expert"), None),
            P(("dp", "expert"), None),
            P(("dp", "expert"), None),
            P(("dp", "expert"), None),
            P(("dp", "expert")),
            P(("dp", "expert")),
            P(),
            P("expert", None, "dp"),
            P("expert", "dp", None),
        ),
        check_vma=False,
    )
```

time: 1410 us -> 1170 us (0.83)
  blocking collectives: 289 us -> 151 us
  waiting for transfers between devices: 556 us -> 443 us
  other arithmetic: 49 us -> 81.2 us
    reduce_scatter x8 -> x1, waiting for transfers between devices: 413 us -> 38 us  [sum_scatter(): part = lax.psum_scatter(values, 'dp', scatter_dimension=0, tiled=True)]
    unnamed x16 -> x15, waiting for transfers between devices: 2.78 us -> 176 us
    all_to_all x4 -> x2, waiting for transfers between devices: 0.01 us -> 136 us  [collect(): lax.all_to_all(sent.reshape(lanes, share, width), 'expert', split_axis=0,...]
    unnamed x2 -> x0, blocking collectives: 82.9 us -> none
    all_gather x8 -> x4, waiting for transfers between devices: 140 us -> 85.9 us  [the longest x1 60 us: local(): dense = lax.all_gather(dense, 'dp', axis=0, tiled=True)]
    all_gather x1 -> x0, blocking collectives: 40.7 us -> none  [local(): lax.all_gather(dense_parts[4], ('dp', 'expert'), axis=0, tiled=True)]
    reduce_sum x7 -> x5, other arithmetic: 4.38 us -> 39.1 us  [the longest x1 25.9 us: local(): table_rows = jnp.sum(grad_scores.astype(f32), axis=0).astype(bf16)]
    add x0 -> x2, local copies, waits for them, and re-layouts: none -> 23.8 us  [attention_scores(): scores * HD ** (-0.5) + bias_grid[None]]
  transfers between devices with their start and end apart: 20 -> 17, of which waited for: 11 -> 11; matrix products, arithmetic and copies ran while one was open for 30% -> 27% of each run, Pallas kernels for 0% -> 0%
where the time goes in v1:
time: 1170 us; the launch traced here: 1160 us
  waiting for transfers between devices  443 us (38%)
  matrix products  284 us (24%)
  local copies, waits for them, and re-layouts  167 us (14%)
  blocking collectives  151 us (13%)
  other arithmetic  81.2 us (7%)
  between operations  16.4 us (1%)
  starting transfers between devices  15.2 us (1%)
    unnamed x15, waiting for transfers between devices  176 us
    all_to_all x2, blocking collectives, dispatch(): lax.all_to_all(buffer.reshape(lanes, share, width), 'expert', split_axis=...  151 us
    all_to_all x2, waiting for transfers between devices, collect(): lax.all_to_all(sent.reshape(lanes, share, width), 'expert', split_axis=0,...  136 us
    unnamed x150, local copies, waits for them, and re-layouts  62 us
    all_gather x1, waiting for transfers between devices, local(): dense = lax.all_gather(dense, 'dp', axis=0, tiled=True)  60 us
    reduce_scatter x1, waiting for transfers between devices, sum_scatter(): part = lax.psum_scatter(values, 'dp', scatter_dimension=0, tiled=True)  38 us
    dot_general x4, matrix products, local(): jnp.einsum('erd,efd->erf', grad_rows, w_out_all[group], preferred_element...  34.6 us
    dot_general x4, matrix products, local(): jnp.einsum('erf,efd->erd', hidden, w_out_all[group], preferred_element_ty...  33.8 us
  transfers between devices with their start and end apart: 17, of which 11 were waited for; matrix products, arithmetic and copies ran while one was open for 27% of the time, Pallas kernels for 0%

profile of v1, /device:TPU:0, one launch (start us, length us, event | category | flops | bytes accessed | tf_op | source)
XLA Modules:
  0.0 1157.2 jit_solution(2598120371002496746)
XLA Ops:
  11.2 25.9 %all-gather.7.cloned.1.call-done = bf16[192,3200]{1,0:T(8,128)(2,1)} async-done(((bf16[24,3200]{1,0:T(8,128)(2,1)}), bf16[192,3200]{1,0:T(8,128)(2,1)}) %all-gather.7.cloned.1.call-update) | async-done | bytes 1228816 | tf_op jit(solution)/shard_map/all_gather | solution.py:114
  37.2 60.0 %all-gather.9.cloned.1.call-done = bf16[768,3200]{1,0:T(8,128)(2,1)} async-done(((bf16[192,3200]{1,0:T(8,128)(2,1)}), bf16[768,3200]{1,0:T(8,128)(2,1)}) %all-gather.9.cloned.1.call-update) | async-done | bytes 4915216 | tf_op jit(solution)/shard_map/all_gather | solution.py:115
  107.8 11.5 fusion.1
  119.4 19.3 %copy.285 = f32[2,8,512,512]{3,2,1,0:T(8,128)} copy(f32[2,8,512,512]{3,1,2,0:T(8,128)S(1)} %bitcast.167) | data formatting | bytes 33554432
  138.7 11.2 slice.140
  149.9 12.6 %copy.221 = f32[12,512,512]{1,2,0:T(8,128)} copy(f32[12,512,512]{2,1,0:T(8,128)} %slice.140) | data formatting | bytes 25165824 | tf_op jit(solution)/shard_map/add | solution.py:62
  166.1 6.4 convolution_convert_fusion
  183.0 3.1 copy.217
  186.2 4.3 reshape.266
  190.5 15.9 %fusion.141 = (f32[2,12,512]{2,1,0:T(8,128)S(1)}, f32[2,12,512,512]{2,3,1,0:T(8,128)}) fusion(f32[12,512,512]{1,2,0:T(8,128)} %copy.221, bf16[2,512,12,64]{1,0,3,2:T(2,128)(2,1)S(1)} %reshape.267, bf16[2,512,12,64]{1,0,3,2:T(2,128)(2,1)} %reshape.266, pred[2,512,512]{1,2,0:T(8,128)(4,1)} %broadcast_compare_fusion), kind=kOutput, calls=%fused_computation.216 | convolution fusion | flops 830459904 | bytes 41467904 | tf_op jit(solution)/shard_map/bphd,bqhd->bhpq/dot_general | solution.py:61
  206.3 11.0 exponential_reduce_fusion
  217.4 10.4 fusion.107
  229.9 3.5 multiply_reduce_fusion.3
  236.2 7.5 scatter_custom_fusion
  243.7 75.9 %all_to_all.20 = bf16[8,256,768]{2,1,0:T(8,128)(2,1)S(1)} all-to-all(bf16[8,256,768]{2,1,0:T(8,128)(2,1)} %bitcast.174), channel_id=1, replica_groups=mesh['dp'=4,'expert'=8] {'expert'}, dimensions={0} | all-to-all | bytes 6291456 | tf_op jit(solution)/shard_map/all_to_all | solution.py:174
  319.8 7.4 fusion.61
  327.2 4.6 fusion.70
  331.8 4.5 fusion.80
  336.2 4.5 fusion.90
  340.8 9.8 fusion.84
  350.5 5.7 fusion.74
  356.2 6.1 fusion.64
  362.3 12.3 %add_convert_fusion.1 = bf16[2,1024,768]{2,1,0:T(8,128)(2,1)S(1)} fusion(f32[2,1024,768]{2,1,0:T(8,128)} %fusion.64, f32[2,1024,768]{2,1,0:T(8,128)} %fusion.84, f32[2,1024,768]{2,1,0:T(8,128)} %fusion.74, bf16[8,768,768]{2,1,0:T(8,128)(2,1)} %all-gather.13.cloned.1.call-done, f32[2,1024,768]{2,1,0:T(8,128)} %fusion.61), kind=kOutput, calls=%fused_computation.63 | convolution fusion | flops 2436366336 | bytes 30670848 | tf_op jit(solution)/shard_map/erf,efd->erd/dot_general | solution.py:202
  376.5 3.7 all-to-all-start.1
  384.6 67.0 %all-to-all-done.1 = bf16[8,256,768]{2,1,0:T(8,128)(2,1)S(1)} async-done(((bf16[8,256,768]{2,1,0:T(8,128)(2,1)}), bf16[8,256,768]{2,1,0:T(8,128)(2,1)S(1)}, u32[]{:S(2)}, u32[]{:S(2)}) %all-to-all-start.1) | async-done | bytes 3145760 | tf_op jit(solution)/shard_map/all_to_all | solution.py:182
  451.6 5.2 gather_fusion
  462.4 7.3 scatter_custom_fusion.1
  469.7 75.3 %all_to_all.21 = bf16[8,256,768]{2,1,0:T(8,128)(2,1)S(1)} all-to-all(bf16[8,256,768]{2,1,0:T(8,128)(2,1)} %bitcast.173), channel_id=1, replica_groups=mesh['dp'=4,'expert'=8] {'expert'}, dimensions={0} | all-to-all | bytes 6291456 | tf_op jit(solution)/shard_map/all_to_all | solution.py:174
  545.3 9.7 fusion.34
  555.1 7.3 fusion.27
  562.4 8.8 fusion.20
  571.2 8.8 fusion.13
  580.0 4.7 fusion.82
  584.7 5.0 fusion.92
  589.7 4.6 fusion.72
  594.3 7.1 add_convert_fusion
  603.2 3.7 all-to-all-start.3
  608.9 69.5 %all-to-all-done.3 = bf16[8,256,768]{2,1,0:T(8,128)(2,1)S(1)} async-done(((bf16[8,256,768]{2,1,0:T(8,128)(2,1)}), bf16[8,256,768]{2,1,0:T(8,128)(2,1)S(1)}, u32[]{:S(2)}, u32[]{:S(2)}) %all-to-all-start.3) | async-done | bytes 3145760 | tf_op jit(solution)/shard_map/all_to_all | solution.py:182
  678.4 5.2 gather_fusion.1
  699.1 11.6 %fusion.104 = bf16[2,512,12,64]{1,3,2,0:T(8,128)(2,1)} fusion(f32[2,12,512,512]{2,3,1,0:T(8,128)} %get-tuple-element.101, f32[2,12,512]{2,1,0:T(8,128)S(1)} %copy-done.31, bf16[2,512,12,64]{1,0,3,2:T(2,128)(2,1)S(1)} %reshape.281), kind=kOutput, calls=%fused_computation.149 | convolution fusion | flops 818675712 | bytes 28360704 | tf_op jit(solution)/shard_map/bhpq,bphd->bqhd/dot_general | solution.py:243
  710.7 19.5 %multiply_reduce_fusion = (f32[2,12,512]{2,1,0:T(8,128)S(1)}, f32[2,12,512,512]{2,3,1,0:T(8,128)}) fusion(f32[2,12,512,512]{2,3,1,0:T(8,128)} %get-tuple-element.101, f32[2,12,512]{2,1,0:T(8,128)S(1)} %copy-done.31, bf16[2,512,12,64]{1,0,3,2:T(2,128)(2,1)S(1)} %copy-done.8, bf16[2,512,12,64]{1,0,3,2:T(2,128)(2,1)S(1)} %reshape.281), kind=kOutput, calls=%fused_computation.8 | convolution fusion | flops 824168448 | bytes 53575680 | tf_op jit(solution)/shard_map/bphd,bqhd->bhpq/dot_general | solution.py:242
  730.3 25.9 %fusion.138 = (bf16[12,512,512]{1,2,0:T(8,128)(2,1)}, bf16[2,12,512,512]{2,3,1,0:T(8,128)(2,1)}) fusion(f32[2,12,512,512]{2,3,1,0:T(8,128)} %get-tuple-element.108, f32[2,12,512]{2,1,0:T(8,128)S(1)} %get-tuple-element.107, f32[2,12,512,512]{2,3,1,0:T(8,128)} %get-tuple-element.101, f32[2,12,512]{2,1,0:T(8,128)S(1)} %copy-done.31), kind=kLoop, calls=%fused_computation.213 | loop fusion | flops 28311552 | bytes 69304320 | tf_op jit(solution)/shard_map/reduce_sum | solution.py:258
  756.2 9.7 fusion.111
  765.9 6.8 fusion.110
  788.0 6.0 fusion.52
  794.3 4.3 convolution_convert_fusion.1
  801.1 9.1 convert_bitcast_fusion
  812.2 9.1 convert_bitcast_fusion.1
  821.3 38.0 %reduce-scatter.15.cloned.1.call-done = bf16[192,2432]{1,0:T(8,128)(2,1)} async-done(((bf16[768,2432]{1,0:T(8,128)(2,1)}), bf16[192,2432]{1,0:T(8,128)(2,1)}) %reduce-scatter.15.cloned.1.call-update) | async-done | bytes 933904 | tf_op jit(solution)/shard_map/reduce_scatter | solution.py:75
  859.6 7.8 convert_bitcast_fusion.2
  867.4 7.0 convert_bitcast_fusion.3
  874.5 4.9 pad_maximum_fusion.1
  879.4 5.7 convert_bitcast_fusion.4
  885.2 3.1 convert_bitcast_fusion.5
  894.2 4.9 pad_maximum_fusion
  899.1 8.7 copy.251
  907.8 6.9 pad.34
  914.7 11.5 copy.292
  926.2 7.8 fusion
  948.6 5.3 fusion.49
  965.7 82.0 %reduce-scatter.23.cloned.1.call-done = bf16[1,2,768,768]{3,2,1,0:T(8,128)(2,1)} async-done(((bf16[4,2,768,768]{3,2,1,0:T(8,128)(2,1)}), bf16[1,2,768,768]{3,2,1,0:T(8,128)(2,1)}) %reduce-scatter.23.cloned.1.call-update) | async-done | bytes 2359312
  1047.7 4.2 bitcast_convert_fusion
  1051.9 93.8 %reduce-scatter.21.cloned.1.call-done = bf16[1,2,768,768]{3,2,1,0:T(8,128)(2,1)} async-done(((bf16[4,2,768,768]{3,2,1,0:T(8,128)(2,1)}), bf16[1,2,768,768]{3,2,1,0:T(8,128)(2,1)}) %reduce-scatter.21.cloned.1.call-update) | async-done | bytes 2359312
  1145.7 4.2 bitcast_convert_fusion.1
  (267 shorter events, 116.8 us)
Async XLA Ops:
  7.2 100.6 %copy-start = (f32[32,12]{0,1:T(8,128)S(1)}, f32[32,12]{0,1:T(8,128)}, u32[]{:S(2)}) copy-start(f32[32,12]{0,1:T(8,128)} %param.25) | copy-start | bytes 4612
  7.2 90.0 %copy-start.43 = (s32[2,3]{1,0:T(2,128)S(1)}, s32[2,3]{1,0:T(2,128)}, u32[]{:S(2)}) copy-start(s32[2,3]{1,0:T(2,128)} %param.16) | copy-start | bytes 76
  7.2 90.9 %copy-start.37 = (s32[1024,1]{0,1:T(1,128)S(1)}, s32[1024,1]{0,1:T(1,128)}, u32[]{:S(2)}) copy-start(s32[1024,1]{0,1:T(1,128)} %param.17) | copy-start | bytes 12292
  7.2 29.9 %all-gather.7.cloned.1.call-start = ((), (), s32[]{:S(2)}) async-start(), calls=%async_computation.9 | async-start | bytes 1382400 | tf_op jit(solution)/shard_map/all_gather | solution.py:114
  11.1 86.0 %all-gather.9.cloned.1.call-start = ((), (), s32[]{:S(2)}) async-start(), calls=%async_computation.10 | async-start | bytes 6144000 | tf_op jit(solution)/shard_map/all_gather | solution.py:115
  37.1 282.7 %all-gather.11.cloned.1.call-start = ((), (), s32[]{:S(2)}) async-start(), calls=%async_computation.12 | async-start | bytes 11796480 | tf_op jit(solution)/shard_map/all_gather | solution.py:117
  97.1 243.6 %all-gather.13.cloned.1.call-start = ((), (), s32[]{:S(2)}) async-start(), calls=%async_computation.13 | async-start | bytes 11796480 | tf_op jit(solution)/shard_map/all_gather | solution.py:118
  105.1 61.1 %copy-start.14 = (bf16[1024,768]{0,1:T(8,128)(2,1)}, bf16[1024,768]{0,1:T(8,128)(2,1)S(1)}, u32[]{:S(2)}) copy-start(bf16[1024,768]{0,1:T(8,128)(2,1)S(1)} %copy.211) | copy-start | bytes 4718596
  107.8 11.5 copy-start.21
  166.1 6.4 copy-start.38
  178.5 38.9 %copy-start.7 = (bf16[2,512,12,64]{1,0,3,2:T(2,128)(2,1)}, bf16[2,512,12,64]{1,0,3,2:T(2,128)(2,1)S(1)}, u32[]{:S(2)}) copy-start(bf16[2,512,12,64]{1,0,3,2:T(2,128)(2,1)S(1)} %reshape.265) | copy-start | bytes 4718596
  183.0 23.3 %copy-start.5 = (bf16[2,512,12,64]{1,0,3,2:T(2,128)(2,1)}, bf16[2,512,12,64]{1,0,3,2:T(2,128)(2,1)S(1)}, u32[]{:S(2)}) copy-start(bf16[2,512,12,64]{1,0,3,2:T(2,128)(2,1)S(1)} %reshape.267) | copy-start | bytes 4718596
  217.4 10.5 copy-start.30
  229.9 3.5 copy-start.32
  235.4 84.1 %copy-start.4 = (bf16[1024,768]{0,1:T(8,128)(2,1)}, bf16[1024,768]{0,1:T(8,128)(2,1)S(1)}, u32[]{:S(2)}) copy-start(bf16[1024,768]{0,1:T(8,128)(2,1)S(1)} %multiply_convert_fusion.7) | copy-start | bytes 4718596
  319.8 16.5 %copy-start.23 = (bf16[2,8,128,768]{3,2,1,0:T(8,128)(2,1)}, bf16[2,8,128,768]{3,2,1,0:T(8,128)(2,1)S(1)}, u32[]{:S(2)}) copy-start(bf16[2,8,128,768]{3,2,1,0:T(8,128)(2,1)S(1)} %copy.227) | copy-start | bytes 9437188
  319.8 7.4 copy-start.35
  340.7 9.8 copy-start.36
  340.8 9.8 copy-start.45
  340.8 15.5 %slice-start.8 = ((s8[6291456]{0:T(1024)(128)(4,1)}), s8[4194304]{0:T(1024)(128)(4,1)S(1)}, s32[]{:S(2)}) async-start(s8[6291456]{0:T(1024)(128)(4,1)} %bitcast.223), calls=%async_computation.27 | async-start | bytes 8388608
  350.5 5.7 slice-start.9
  376.5 75.1 %all-to-all-start.1 = ((bf16[8,256,768]{2,1,0:T(8,128)(2,1)}), bf16[8,256,768]{2,1,0:T(8,128)(2,1)S(1)}, u32[]{:S(2)}, u32[]{:S(2)}) async-start(bf16[8,256,768]{2,1,0:T(8,128)(2,1)} %bitcast.171), calls=%async_computation.1 | async-start | bytes 6291456 | tf_op jit(solution)/shard_map/all_to_all | solution.py:182
  458.7 3.7 copy-start.12
  545.0 10.0 slice-start.3
  545.0 10.0 slice-start.10
  545.2 26.0 %copy-start.25 = (bf16[2,8,128,768]{3,2,1,0:T(8,128)(2,1)}, bf16[2,8,128,768]{3,2,1,0:T(8,128)(2,1)S(1)}, u32[]{:S(2)}) copy-start(bf16[2,8,128,768]{3,2,1,0:T(8,128)(2,1)S(1)} %copy.232) | copy-start | bytes 9437188
  545.3 9.7 slice-start.4
  545.3 9.7 slice-start.5
  545.3 9.7 slice-start.11
  555.0 39.2 %copy-start.27 = (bf16[2,1024,768]{2,1,0:T(8,128)(2,1)}, bf16[2,1024,768]{2,1,0:T(8,128)(2,1)S(1)}, u32[]{:S(2)}) copy-start(bf16[2,1024,768]{2,1,0:T(8,128)(2,1)S(1)} %fusion.34) | copy-start | bytes 9437188
  562.4 17.6 %slice-start = ((s8[9437184]{0:T(1024)(128)(4,1)}), s8[4194304]{0:T(1024)(128)(4,1)S(1)}, s32[]{:S(2)}) async-start(s8[9437184]{0:T(1024)(128)(4,1)} %bitcast.206), calls=%async_computation.19 | async-start | bytes 8388608
  562.4 17.6 %slice-start.1 = ((s8[9437184]{0:T(1024)(128)(4,1)}), s8[4194304]{0:T(1024)(128)(4,1)S(1)}, s32[]{:S(2)}) async-start(s8[9437184]{0:T(1024)(128)(4,1)} %bitcast.206), calls=%async_computation.20 | async-start | bytes 8388608
  571.2 8.8 slice-start.2
  580.0 4.7 copy-start.49
  584.7 5.0 copy-start.47
  603.2 75.1 %all-to-all-start.3 = ((bf16[8,256,768]{2,1,0:T(8,128)(2,1)}), bf16[8,256,768]{2,1,0:T(8,128)(2,1)S(1)}, u32[]{:S(2)}, u32[]{:S(2)}) async-start(bf16[8,256,768]{2,1,0:T(8,128)(2,1)} %bitcast.172), calls=%async_computation.3 | async-start | bytes 6291456 | tf_op jit(solution)/shard_map/all_to_all | solution.py:182
  606.9 203.3 %reduce-scatter.17.cloned.1.call-start = ((), (), s32[]{:S(2)}) async-start(), calls=%async_computation.14 | async-start | bytes 1720320
  686.3 2.9 copy-start.13
  699.1 11.6 %copy-start.8 = (bf16[2,512,12,64]{1,0,3,2:T(2,128)(2,1)S(1)}, bf16[2,512,12,64]{1,0,3,2:T(2,128)(2,1)}, u32[]{:S(2)}) copy-start(bf16[2,512,12,64]{1,0,3,2:T(2,128)(2,1)} %copy-done.7) | copy-start | bytes 4718596
  730.3 25.9 %copy-start.9 = (bf16[2,512,12,64]{1,0,3,2:T(2,128)(2,1)S(1)}, bf16[2,512,12,64]{1,0,3,2:T(2,128)(2,1)}, u32[]{:S(2)}) copy-start(bf16[2,512,12,64]{1,0,3,2:T(2,128)(2,1)} %reshape.266) | copy-start | bytes 4718596
  756.2 9.7 copy-start.6
  765.9 6.8 copy-start.34
  773.9 5.2 copy-start.19
  779.1 80.2 %reduce-scatter.15.cloned.1.call-start = ((), (), s32[]{:S(2)}) async-start(), calls=%async_computation.11 | async-start | bytes 4669440 | tf_op jit(solution)/shard_map/reduce_scatter | solution.py:75
  800.6 159.0 %all-reduce.9.cloned.1.call-start = ((), (), s32[]{:S(2)}) async-start(), calls=%async_computation.15 | async-start | bytes 917504
  812.2 150.5 %reduce-scatter.19.cloned.1.call-start = ((), (), s32[]{:S(2)}) async-start(), calls=%async_computation.16 | async-start | bytes 1050624
  859.3 188.4 %reduce-scatter.23.cloned.1.call-start = ((), (), s32[]{:S(2)}) async-start(), calls=%async_computation.18 | async-start | bytes 11796480
  859.6 7.9 copy-start.26
  867.4 7.0 copy-start.28
  867.4 7.0 copy-start.29
  879.4 266.4 %reduce-scatter.21.cloned.1.call-start = ((), (), s32[]{:S(2)}) async-start(), calls=%async_computation.17 | async-start | bytes 11796480
  879.4 5.7 copy-start.24
  879.4 5.7 copy-start.48
  885.2 3.1 copy-start.50
  888.3 2.9 copy-start.46
  914.7 11.5 copy-start.22
  926.2 15.1 %copy-start.44 = (u32[32]{0:T(128)S(1)}, u32[32]{0:T(128)}, u32[]{:S(2)}) copy-start(u32[32]{0:T(128)} %constant.92) | copy-start | bytes 388
  926.2 22.5 %copy-start.40 = (f32[1024]{0:T(1024)S(1)}, f32[1024]{0:T(1024)}, u32[]{:S(2)}) copy-start(f32[1024]{0:T(1024)} %get-tuple-element.96) | copy-start | bytes 12292
  934.0 1.2 collective-permute-start
  935.1 3.7 collective-permute-start.1
  938.8 4.7 collective-permute-start.2
  943.5 3.7 collective-permute-start.3
  947.1 11.9 %collective-permute-start.4 = (f32[32,12]{0,1:T(8,128)S(1)}, f32[32,12]{0,1:T(8,128)S(1)}, u32[]{:S(2)}, u32[]{:S(2)}) collective-permute-start(f32[32,12]{0,1:T(8,128)S(1)} %add.285), channel_id=1, source_target_pairs={{0,16},{1,17},{2,18},{3,19},{4,20},{5,21},{6,22},{7,23},{8,24},{9,... | collective-permute-start | bytes 4616 | tf_op jit(solution)/shard_map/ppermute | solution.py:69
  1047.7 102.2 %copy-start.1 = (f32[32,12]{0,1:T(8,128)S(1)}, f32[32,12]{0,1:T(8,128)}, u32[]{:S(2)}) copy-start(f32[32,12]{0,1:T(8,128)} %param.25) | copy-start | bytes 4612
  (16 other events, 38.1 us)
Sparse Core Ops, SparseCore 0:
  11.3 25.7 all-gather.6
  38.9 58.1 all-gather.8
  99.0 96.3 all-gather.10
  197.1 96.3 all-gather.12
  779.2 27.6 reduce-scatter.16
  810.4 48.8 reduce-scatter.14
  861.6 55.8 all-reduce.8
  919.9 31.5 reduce-scatter.18
  954.6 93.0 reduce-scatter.22
  1050.7 95.0 reduce-scatter.20

commit v2 on v1

--- a/solution.py
+++ b/solution.py
@@ -1,6 +1,8 @@
 import jax
 import jax.numpy as jnp
 from jax import lax
+from jax.experimental import pallas as pl
+from jax.experimental.pallas import tpu as pltpu
 from jax.sharding import PartitionSpec as P
 
 H = 12
@@ -55,6 +57,31 @@
     return lax.dot_general(
         former, latter, (((1,), (1,)), ((), ())), preferred_element_type=jnp.float32
     )
+
+
+def bias_kernel(line_ref, grid_ref):
+    extent = grid_ref.shape[1]
+    wide = jnp.broadcast_to(line_ref[0], (extent, 2 * extent))
+    turned = pltpu.roll(wide, extent + 1, 1, stride=1, stride_axis=0)
+    grid_ref[0] = turned[:, :extent]
+
+
+def bias_of_offsets(bias_table, extent):
+    offset = jnp.arange(2 * extent, dtype=jnp.int32) - (extent - 1)
+    spread = jnp.abs(offset)
+    beyond = 8 + sum(((spread >= threshold).astype(jnp.int32) for threshold in THRESHOLDS))
+    bucket = jnp.where(offset > 0, 16, 0) + jnp.where(spread < 8, spread, beyond)
+    hot = (jnp.arange(bias_table.shape[0], dtype=jnp.int32)[:, None] == bucket[None, :])
+    line = jnp.sum(bias_table[:, :, None] * hot.astype(jnp.float32)[:, None, :], axis=0)
+    return pl.pallas_call(
+        bias_kernel,
+        grid=(H,),
+        in_specs=[pl.BlockSpec((1, 1, 2 * extent), lambda h: (h, 0, 0))],
+        out_specs=pl.BlockSpec((1, extent, extent), lambda h: (h, 0, 0)),
+        out_shape=jax.ShapeDtypeStruct((H, extent, extent), jnp.float32),
+        compiler_params=pltpu.CompilerParams(vmem_limit_bytes=32 * 1024 * 1024),
+        name="bias_grid",
+    )(line[:, None, :])
 
 
 def attention_scores(query, key, bias_grid, allowed):
@@ -116,21 +143,35 @@
     dense, w_in, w_out = lax.optimization_barrier((dense, w_in, w_out))
     w_in_all = lax.all_gather(w_in, "dp", axis=0, tiled=False)
     w_out_all = lax.all_gather(w_out, "dp", axis=0, tiled=False)
+    bucket_flat = bucket_grid(extent).reshape(1, extent * extent)
+    bucket_hot = (jnp.arange(bucket_count, dtype=jnp.int32)[:, None] == bucket_flat)
+    bias_grid = bias_of_offsets(bias_table, extent)
+    choose = (routes == jnp.arange(expert_total, dtype=jnp.int32)[None, :]).astype(jnp.int32)
+    by_block = choose.reshape(blocks, extent, expert_total)
+    slot = jnp.sum(jnp.cumsum(by_block, axis=1) * by_block, axis=-1) - 1
+    place = (
+        routes[:, 0].reshape(blocks, extent) * (blocks * capacity)
+        + jnp.arange(blocks, dtype=jnp.int32)[:, None] * capacity
+        + slot
+    ).reshape(rows)
+
+    share = expert_local * blocks * capacity
+
+    def dispatch(values):
+        buffer = jnp.zeros((expert_total * blocks * capacity, width), bf16).at[place].set(values)
+        got = lax.all_to_all(
+            buffer.reshape(lanes, share, width), "expert", split_axis=0, concat_axis=0, tiled=True
+        )
+        got = got.reshape(lanes, expert_local, blocks * capacity, width)
+        return got.transpose(1, 0, 2, 3).reshape(expert_local, lanes * blocks * capacity, width)
+
+    gained_rows = dispatch(cotangent)
+    dense, bias_grid, gained_rows = lax.optimization_barrier((dense, bias_grid, gained_rows))
     weight_qkv = dense[:, : 3 * width]
     weight_output = dense[:, 3 * width : 4 * width]
     router_full = dense[:, 4 * width : 4 * width + expert_total]
     gain_one = dense[:, 4 * width + expert_total].astype(f32)
     gain_two = dense[:, 4 * width + expert_total + 1].astype(f32)
-
-    bucket_flat = bucket_grid(extent).reshape(1, extent * extent)
-    bucket_hot = (jnp.arange(bucket_count, dtype=jnp.int32)[:, None] == bucket_flat)
-    bias_grid = lax.dot_general(
-        bias_table,
-        bucket_hot.astype(f32),
-        (((0,), (0,)), ((), ())),
-        precision=lax.Precision.HIGHEST,
-        preferred_element_type=f32,
-    ).reshape(H, extent, extent)
     allowed = jax.vmap(lambda own: same_sequence(own, extent))(lengths)
 
     rows_in = tokens.astype(f32)
@@ -154,88 +195,80 @@
     logits = jnp.dot(second, router_full, preferred_element_type=f32)
     exps = jnp.exp(logits - jnp.max(logits, axis=-1, keepdims=True))
     gate_probs = exps / jnp.sum(exps, axis=-1, keepdims=True)
-    choose = (routes == jnp.arange(expert_total, dtype=jnp.int32)[None, :]).astype(jnp.int32)
-    by_block = choose.reshape(blocks, extent, expert_total)
-    slot = jnp.sum(jnp.cumsum(by_block, axis=1) * by_block, axis=-1) - 1
-    place = (
-        routes[:, 0].reshape(blocks, extent) * (blocks * capacity)
-        + jnp.arange(blocks, dtype=jnp.int32)[:, None] * capacity
-        + slot
-    ).reshape(rows)
     choose_float = choose.astype(f32)
     gate = jnp.sum(gate_probs * choose_float, axis=-1, keepdims=True)
     final = cotangent.astype(f32)
-    grad_expert = (gate * final).astype(bf16)
-
-    share = expert_local * blocks * capacity
-
-    def dispatch(values):
-        buffer = jnp.zeros((expert_total * blocks * capacity, width), bf16).at[place].set(values)
-        got = lax.all_to_all(
-            buffer.reshape(lanes, share, width), "expert", split_axis=0, concat_axis=0, tiled=True
-        )
-        got = got.reshape(lanes, expert_local, blocks * capacity, width)
-        return got.transpose(1, 0, 2, 3).reshape(expert_local, lanes * blocks * capacity, width)
-
-    def collect(values):
+    def collect_start(values):
         sent = values.reshape(expert_local, lanes, blocks * capacity, width).transpose(1, 0, 2, 3)
         got = lax.all_to_all(
             sent.reshape(lanes, share, width), "expert", split_axis=0, concat_axis=0, tiled=True
         )
-        return got.reshape(expert_total * blocks * capacity, width)[place].astype(f32)
+        return got.reshape(expert_total * blocks * capacity, width)
+
+    def collect(values):
+        return collect_start(values)[place].astype(f32)
 
     expert_rows = dispatch(second)
-    grad_rows = dispatch(grad_expert)
-
+    gained = gained_rows.astype(f32)
+    row_logits = jnp.einsum("erd,dk->erk", expert_rows, router_full, preferred_element_type=f32)
+    row_exps = jnp.exp(row_logits - jnp.max(row_logits, axis=-1, keepdims=True))
+    row_probs = row_exps / jnp.sum(row_exps, axis=-1, keepdims=True)
+    own_expert = lax.axis_index("expert") * expert_local + jnp.arange(expert_local, dtype=jnp.int32)
+    own_hot = (own_expert[:, None] == jnp.arange(expert_total, dtype=jnp.int32)[None, :])
+    own_hot = own_hot.astype(f32)[:, None, :]
+    row_gate = jnp.sum(row_probs * own_hot, axis=-1, keepdims=True)
+    grad_rows = (row_gate * gained).astype(bf16)
+
+    pres = []
+    hiddens = []
+    for group in range(groups):
+        pre = jnp.einsum("erd,edf->erf", expert_rows, w_in_all[group], preferred_element_type=f32)
+        pres.append(pre)
+        hiddens.append(gelu_tanh(pre).astype(bf16))
+    grad_out_parts = jnp.stack(
+        [
+            jnp.einsum("erf,erd->efd", own, grad_rows, preferred_element_type=f32).astype(bf16)
+            for own in hiddens
+        ]
+    )
+    grad_out_parts, hiddens = lax.optimization_barrier((grad_out_parts, hiddens))
+    grad_out = lax.psum_scatter(grad_out_parts, "dp", scatter_dimension=0, tiled=True)
     out_total = 0.0
-    back_total = 0.0
-    hiddens = []
+    for group in range(groups):
+        out_total = out_total + jnp.einsum(
+            "erf,efd->erd", hiddens[group], w_out_all[group], preferred_element_type=f32
+        )
+    out_low = out_total.astype(bf16)
+    expert_out = collect(out_low)
+    row_grad_gate = jnp.sum(gained * out_low.astype(f32), axis=-1, keepdims=True)
+    grad_logits = (row_probs * (own_hot * row_grad_gate - row_gate * row_grad_gate)).astype(bf16)
+    grad_router = jnp.einsum("erd,erk->dk", expert_rows, grad_logits, preferred_element_type=f32)
+    back_total = jnp.einsum("erk,dk->erd", grad_logits, router_full, preferred_element_type=f32)
     grad_pres = []
     for group in range(groups):
-        pre = jnp.einsum("erd,edf->erf", expert_rows, w_in_all[group], preferred_element_type=f32)
         grad_hidden = jnp.einsum(
             "erd,efd->erf", grad_rows, w_out_all[group], preferred_element_type=f32
         )
-        activated, pull = jax.vjp(gelu_tanh, pre)
-        hidden = activated.astype(bf16)
-        grad_pre = pull(grad_hidden)[0].astype(bf16)
-        out_total = out_total + jnp.einsum(
-            "erf,efd->erd", hidden, w_out_all[group], preferred_element_type=f32
-        )
+        grad_pre = jax.vjp(gelu_tanh, pres[group])[1](grad_hidden)[0].astype(bf16)
         back_total = back_total + jnp.einsum(
             "erf,edf->erd", grad_pre, w_in_all[group], preferred_element_type=f32
         )
-        hiddens.append(hidden)
         grad_pres.append(grad_pre)
-    expert_out = collect(out_total.astype(bf16))
-    grad_second = collect(back_total.astype(bf16))
+    back_low = collect_start(back_total.astype(bf16))
     grad_in_parts = jnp.stack(
         [
             jnp.einsum("erd,erf->edf", expert_rows, own, preferred_element_type=f32).astype(bf16)
             for own in grad_pres
         ]
     )
+    back_low, grad_in_parts = lax.optimization_barrier((back_low, grad_in_parts))
     grad_in = lax.psum_scatter(grad_in_parts, "dp", scatter_dimension=0, tiled=True)
-    grad_out_parts = jnp.stack(
-        [
-            jnp.einsum("erf,erd->efd", own, grad_rows, preferred_element_type=f32).astype(bf16)
-            for own in hiddens
-        ]
-    )
-    grad_out = lax.psum_scatter(grad_out_parts, "dp", scatter_dimension=0, tiled=True)
+    grad_second = back_low[place].astype(f32)
 
     block_out = (middle + gate * expert_out).astype(bf16)
-    grad_gate = jnp.sum(final * expert_out, axis=-1, keepdims=True)
-    grad_logits = (gate_probs * (choose_float * grad_gate - gate * grad_gate)).astype(bf16)
-    grad_router = contract_rows(second, grad_logits)
-    grad_second = grad_second + contract_cols(grad_logits, router_full)
     grad_part, grad_gain_two = rms_backward(middle, scale_two, gain_two, grad_second)
     grad_middle = final + grad_part
     grad_attended = grad_middle.astype(bf16)
-    early = lane_padded(
-        (contract_rows(context, grad_attended), grad_router, grad_gain_two[:, None])
-    ).astype(bf16)
-    early = sum_scatter(early).astype(f32)
     grad_context = contract_cols(grad_attended, weight_output).astype(bf16).reshape(shape)
 
     soft = jnp.exp(attention_scores(query, key, bias_grid, allowed) - log_total)
@@ -266,18 +299,26 @@
     grad_normed = contract_cols(grad_qkv, weight_qkv)
     grad_part, grad_gain_one = rms_backward(rows_in, scale_one, gain_one, grad_normed)
     grad_tokens = grad_middle + grad_part
-    late = lane_padded((contract_rows(normed, grad_qkv), grad_gain_one[:, None])).astype(bf16)
-    late = sum_scatter(late).astype(f32)
+    sums = lane_padded(
+        (
+            contract_rows(normed, grad_qkv),
+            contract_rows(context, grad_attended),
+            grad_router,
+            grad_gain_one[:, None],
+            grad_gain_two[:, None],
+        )
+    ).astype(bf16)
+    sums = sum_scatter(sums).astype(f32)
     return (
         block_out,
         grad_tokens,
-        late[:, :width],
-        late[:, width : 2 * width],
-        late[:, 2 * width : 3 * width],
-        early[:, :width],
-        early[:, width : width + expert_total],
-        late[:, 3 * width],
-        early[:, width + expert_total],
+        sums[:, :width],
+        sums[:, width : 2 * width],
+        sums[:, 2 * width : 3 * width],
+        sums[:, 3 * width : 4 * width],
+        sums[:, 4 * width : 4 * width + expert_total],
+        sums[:, 4 * width + expert_total],
+        sums[:, 4 * width + expert_total + 1],
         grad_table,
         grad_in.astype(f32).reshape(w_in.shape),
         grad_out.astype(f32).reshape(w_out.shape),

time: 1170 us -> 1080 us (0.923)
  blocking collectives: 151 us -> 0 us
  waiting for transfers between devices: 443 us -> 535 us
  matrix products: 284 us -> 250 us
    all_to_all x2 -> x0, blocking collectives: 151 us -> none  [dispatch(): lax.all_to_all(buffer.reshape(lanes, share, width), 'expert', split_axis=...]
    all_to_all x2 -> x4, waiting for transfers between devices: 136 us -> 222 us  [the longest x2 124 us: dispatch(): lax.all_to_all(buffer.reshape(lanes, share, width), 'expert', split_axis=...]
    add x2 -> x0, local copies, waits for them, and re-layouts: 23.8 us -> none  [attention_scores(): scores * HD ** (-0.5) + bias_grid[None]]
    optimization_barrier x0 -> x2, local copies, waits for them, and re-layouts: none -> 20.7 us  [local(): lax.optimization_barrier((dense, bias_grid, gained_rows))]
    reduce_scatter x1, waiting for transfers between devices: 38 us -> 56.7 us  [sum_scatter(): part = lax.psum_scatter(values, 'dp', scatter_dimension=0, tiled=True)]
    dot_general x4, matrix products: 33.1 us -> 14.9 us  [local(): jnp.einsum('erf,erd->efd', own, grad_rows, preferred_element_type=f32)]
    unnamed x150 -> x158, local copies, waits for them, and re-layouts: 62 us -> 47.6 us
    unnamed x15 -> x11, waiting for transfers between devices: 176 us -> 163 us
  transfers between devices with their start and end apart: 17 -> 17, of which waited for: 11 -> 13; matrix products, arithmetic and copies ran while one was open for 27% -> 24% of each run, Pallas kernels for 0% -> 0%
where the time goes in v2:
time: 1080 us
  waiting for transfers between devices  535 us (50%)
  matrix products  250 us (23%)
  local copies, waits for them, and re-layouts  171 us (16%)
  other arithmetic  76.5 us (7%)
  starting transfers between devices  23 us (2%)
  between operations  15.8 us (1%)
    unnamed x11, waiting for transfers between devices  163 us
    all_to_all x2, waiting for transfers between devices, dispatch(): lax.all_to_all(buffer.reshape(lanes, share, width), 'expert', split_axis=...  124 us
    all_to_all x2, waiting for transfers between devices, collect_start(): lax.all_to_all(sent.reshape(lanes, share, width), 'expert', split_axis=0,...  97.9 us
    all_gather x1, waiting for transfers between devices, local(): dense = lax.all_gather(dense, 'dp', axis=0, tiled=True)  60 us
    reduce_scatter x1, waiting for transfers between devices, sum_scatter(): part = lax.psum_scatter(values, 'dp', scatter_dimension=0, tiled=True)  56.7 us
    unnamed x158, local copies, waits for them, and re-layouts  47.6 us
    dot_general x4, matrix products, local(): jnp.einsum('erd,efd->erf', grad_rows, w_out_all[group], preferred_element...  36.6 us
    all_gather x1, waiting for transfers between devices, local(): dense = lax.all_gather(packed, 'expert', axis=0, tiled=True)  25.9 us
  transfers between devices with their start and end apart: 17, of which 13 were waited for; matrix products, arithmetic and copies ran while one was open for 24% of the time, Pallas kernels for 0%

profile of v2, /device:TPU:0, one launch (start us, length us, event | category | flops | bytes accessed | tf_op | source)
XLA Modules:
  0.0 1075.1 jit_solution(5188733036794774878)
XLA Ops:
  11.2 25.9 %all-gather.7.cloned.1.call-done = bf16[192,3200]{1,0:T(8,128)(2,1)} async-done(((bf16[24,3200]{1,0:T(8,128)(2,1)}), bf16[192,3200]{1,0:T(8,128)(2,1)}) %all-gather.7.cloned.1.call-update) | async-done | bytes 1228816 | tf_op jit(solution)/shard_map/all_gather | solution.py:141
  37.1 60.0 %all-gather.9.cloned.1.call-done = bf16[768,3200]{1,0:T(8,128)(2,1)} async-done(((bf16[192,3200]{1,0:T(8,128)(2,1)}), bf16[768,3200]{1,0:T(8,128)(2,1)}) %all-gather.9.cloned.1.call-update) | async-done | bytes 4915216 | tf_op jit(solution)/shard_map/all_gather | solution.py:142
  101.2 7.9 scatter_custom_fusion
  109.1 4.7 all-to-all-start
  117.1 4.6 copy-done
  124.9 60.6 %all-to-all-done = bf16[8,256,768]{2,1,0:T(8,128)(2,1)} async-done(((bf16[8,256,768]{2,1,0:T(8,128)(2,1)}), bf16[8,256,768]{2,1,0:T(8,128)(2,1)}, u32[]{:S(2)}, u32[]{:S(2)}) %all-to-all-start) | async-done | bytes 3145760 | tf_op jit(solution)/shard_map/all_to_all | solution.py:162
  185.5 3.8 copy.282
  191.3 6.4 convolution_convert_fusion
  201.7 3.8 reshape.345
  210.0 13.2 %copy.289 = f32[12,512,512]{1,2,0:T(8,128)} copy(f32[12,512,512]{2,1,0:T(8,128)} %copy-done) | data formatting | bytes 25165824 | tf_op jit(solution)/shard_map/optimization_barrier | solution.py:169
  227.8 15.0 %fusion.168 = (f32[2,12,512]{2,1,0:T(8,128)S(1)}, f32[2,12,512,512]{2,3,1,0:T(8,128)}) fusion(f32[12,512,512]{1,2,0:T(8,128)} %copy.289, bf16[2,512,12,64]{1,0,3,2:T(2,128)(2,1)S(1)} %reshape.346, bf16[2,512,12,64]{1,0,3,2:T(2,128)(2,1)} %reshape.345, pred[2,512,512]{1,2,0:T(8,128)(4,1)} %broadcast_compare_fusion), kind=kOutput, calls=%fused_computation.238 | convolution fusion | flops 830459904 | bytes 41467904 | tf_op jit(solution)/shard_map/bphd,bqhd->bhpq/dot_general | solution.py:88
  242.8 10.1 exponential_reduce_fusion
  252.9 10.9 %fusion.109 = bf16[2,512,12,64]{1,3,2,0:T(8,128)(2,1)S(1)} fusion(f32[2,12,512,512]{2,3,1,0:T(8,128)} %get-tuple-element.134, f32[2,12,512]{2,1,0:T(8,128)S(1)} %log_add_fusion, bf16[2,512,12,64]{1,0,3,2:T(2,128)(2,1)S(1)} %reshape.344), kind=kOutput, calls=%fused_computation.150 | convolution fusion | flops 818675712 | bytes 28360704 | tf_op jit(solution)/shard_map/bhpq,bqhd->bphd/dot_general | solution.py:189
  272.6 7.3 scatter_custom_fusion.1
  279.9 3.8 all-to-all-start.1
  283.9 7.5 copy.293
  291.3 63.9 %all-to-all-done.1 = bf16[8,256,768]{2,1,0:T(8,128)(2,1)S(1)} async-done(((bf16[8,256,768]{2,1,0:T(8,128)(2,1)}), bf16[8,256,768]{2,1,0:T(8,128)(2,1)S(1)}, u32[]{:S(2)}, u32[]{:S(2)}) %all-to-all-start.1) | async-done | bytes 3145760 | tf_op jit(solution)/shard_map/all_to_all | solution.py:162
  361.4 7.2 multiply_convert_fusion.4
  372.0 5.6 multiply_convert_fusion.3
  377.6 5.0 convert_bitcast_fusion.6
  382.6 5.2 multiply_convert_fusion.2
  392.8 5.6 multiply_convert_fusion.1
  401.7 4.9 pad_maximum_fusion
  406.6 5.4 fusion.68
  412.9 4.5 fusion.74
  417.4 4.5 fusion.62
  421.9 8.2 fusion.5
  430.1 8.2 fusion.12
  438.4 9.5 fusion.19
  447.9 8.9 fusion.26
  456.8 10.0 fusion.33
  466.9 4.6 fusion.94
  471.4 4.6 fusion.90
  476.0 4.5 fusion.86
  480.6 4.6 fusion.82
  485.1 9.8 add_convert_fusion
  496.8 3.7 all-to-all-start.3
  500.4 3.8 copy.300
  504.2 67.6 %all-to-all-done.3 = bf16[8,256,768]{2,1,0:T(8,128)(2,1)S(1)} async-done(((bf16[8,256,768]{2,1,0:T(8,128)(2,1)}), bf16[8,256,768]{2,1,0:T(8,128)(2,1)S(1)}, u32[]{:S(2)}, u32[]{:S(2)}) %all-to-all-start.3) | async-done | bytes 3145760 | tf_op jit(solution)/shard_map/all_to_all | solution.py:203
  584.6 5.7 convert_bitcast_fusion.3
  599.6 4.9 pad_maximum_fusion.1
  604.5 7.9 gather_fusion.1
  618.4 30.3 %all-to-all-done.2 = bf16[8,256,768]{2,1,0:T(8,128)(2,1)S(1)} async-done(((bf16[8,256,768]{2,1,0:T(8,128)(2,1)}), bf16[8,256,768]{2,1,0:T(8,128)(2,1)S(1)}, u32[]{:S(2)}, u32[]{:S(2)}) %all-to-all-start.2) | async-done | bytes 3145760 | tf_op jit(solution)/shard_map/all_to_all | solution.py:203
  648.7 5.2 gather_fusion
  657.0 5.0 fusion.41
  671.0 19.5 %multiply_reduce_fusion = (f32[2,12,512]{2,1,0:T(8,128)S(1)}, f32[2,12,512,512]{2,3,1,0:T(8,128)}) fusion(f32[2,12,512,512]{2,3,1,0:T(8,128)} %get-tuple-element.134, f32[2,12,512]{2,1,0:T(8,128)S(1)} %copy-done.26, bf16[2,512,12,64]{1,0,3,2:T(2,128)(2,1)S(1)} %copy-done.9, bf16[2,512,12,64]{1,0,3,2:T(2,128)(2,1)S(1)} %reshape.356), kind=kOutput, calls=%fused_computation.8 | convolution fusion | flops 824168448 | bytes 53575680 | tf_op jit(solution)/shard_map/bphd,bqhd->bhpq/dot_general | solution.py:275
  690.5 10.4 fusion.106
  700.9 25.7 %fusion.165 = (bf16[12,512,512]{1,2,0:T(8,128)(2,1)}, bf16[2,12,512,512]{2,3,1,0:T(8,128)(2,1)}) fusion(f32[2,12,512,512]{2,3,1,0:T(8,128)} %get-tuple-element.152, f32[2,12,512]{2,1,0:T(8,128)S(1)} %get-tuple-element.151, f32[2,12,512,512]{2,3,1,0:T(8,128)} %get-tuple-element.134, f32[2,12,512]{2,1,0:T(8,128)S(1)} %copy-done.26), kind=kLoop, calls=%fused_computation.235 | loop fusion | flops 28311552 | bytes 69304320 | tf_op jit(solution)/shard_map/reduce_sum | solution.py:291
  726.6 8.6 fusion.113
  735.2 6.9 fusion.112
  751.2 5.7 convolution_convert_fusion.1
  756.9 5.8 fusion.53
  763.0 8.1 concatenate.12
  771.2 4.9 pad.10
  776.1 56.7 %reduce-scatter.11.cloned.1.call-done = bf16[192,3200]{1,0:T(8,128)(2,1)} async-done(((bf16[768,3200]{1,0:T(8,128)(2,1)}), bf16[192,3200]{1,0:T(8,128)(2,1)}) %reduce-scatter.11.cloned.1.call-update) | async-done | bytes 1228816 | tf_op jit(solution)/shard_map/reduce_scatter | solution.py:102
  836.1 8.9 copy.327
  845.0 6.7 pad.21
  851.7 11.4 %copy.354 = bf16[2,8,512,512]{3,1,2,0:T(8,128)(2,1)} copy(bf16[2,8,512,512]{3,2,1,0:T(8,128)(2,1)} %bitcast.168) | data formatting | bytes 16777216
  863.2 7.7 fusion.1
  887.9 3.7 copy.329
  898.3 67.1 %reduce-scatter.17.cloned.1.call-done = bf16[1,2,768,768]{3,2,1,0:T(8,128)(2,1)} async-done(((bf16[4,2,768,768]{3,2,1,0:T(8,128)(2,1)}), bf16[1,2,768,768]{3,2,1,0:T(8,128)(2,1)}) %reduce-scatter.17.cloned.1.call-update) | async-done | bytes 2359312
  965.4 4.2 bitcast_convert_fusion
  969.6 94.0 %reduce-scatter.15.cloned.1.call-done = bf16[1,2,768,768]{3,2,1,0:T(8,128)(2,1)} async-done(((bf16[4,2,768,768]{3,2,1,0:T(8,128)(2,1)}), bf16[1,2,768,768]{3,2,1,0:T(8,128)(2,1)}) %reduce-scatter.15.cloned.1.call-update) | async-done | bytes 2359312
  1063.6 4.2 bitcast_convert_fusion.1
  (275 shorter events, 135.0 us)
Async XLA Ops:
  7.2 89.9 %copy-start.35 = (s32[1024,1]{0,1:T(1,128)S(1)}, s32[1024,1]{0,1:T(1,128)}, u32[]{:S(2)}) copy-start(s32[1024,1]{0,1:T(1,128)} %param.17) | copy-start | bytes 12292
  7.2 29.9 %all-gather.7.cloned.1.call-start = ((), (), s32[]{:S(2)}) async-start(), calls=%async_computation.8 | async-start | bytes 1382400 | tf_op jit(solution)/shard_map/all_gather | solution.py:141
  11.1 86.0 %all-gather.9.cloned.1.call-start = ((), (), s32[]{:S(2)}) async-start(), calls=%async_computation.9 | async-start | bytes 6144000 | tf_op jit(solution)/shard_map/all_gather | solution.py:142
  37.1 324.3 %all-gather.11.cloned.1.call-start = ((), (), s32[]{:S(2)}) async-start(), calls=%async_computation.11 | async-start | bytes 11796480 | tf_op jit(solution)/shard_map/all_gather | solution.py:144
  101.2 171.4 %copy-start.43 = (s32[1024,1]{0,1:T(1,128)}, s32[1024,1]{0,1:T(1,128)S(1)}, u32[]{:S(2)}) copy-start(s32[1024,1]{0,1:T(1,128)S(1)} %compare_select_fusion.1) | copy-start | bytes 12292
  109.1 5.0 copy-start.45
  109.1 76.4 %all-to-all-start = ((bf16[8,256,768]{2,1,0:T(8,128)(2,1)}), bf16[8,256,768]{2,1,0:T(8,128)(2,1)}, u32[]{:S(2)}, u32[]{:S(2)}) async-start(bf16[8,256,768]{2,1,0:T(8,128)(2,1)} %bitcast.5), calls=%async_computation | async-start | bytes 6291456 | tf_op jit(solution)/shard_map/all_to_all | solution.py:162
  113.9 292.7 %all-gather.13.cloned.1.call-start = ((), (), s32[]{:S(2)}) async-start(), calls=%async_computation.12 | async-start | bytes 11796480 | tf_op jit(solution)/shard_map/all_gather | solution.py:145
  114.5 7.1 copy-start.27
  117.1 4.6 copy-start
  122.4 68.3 %copy-start.12 = (bf16[1024,768]{0,1:T(8,128)(2,1)}, bf16[1024,768]{0,1:T(8,128)(2,1)S(1)}, u32[]{:S(2)}) copy-start(bf16[1024,768]{0,1:T(8,128)(2,1)S(1)} %copy.277) | copy-start | bytes 4718596
  123.8 67.0 %copy-start.40 = (f32[1024]{0:T(1024)}, f32[1024]{0:T(1024)S(1)}, u32[]{:S(2)}) copy-start(f32[1024]{0:T(1024)S(1)} %get-tuple-element.130) | copy-start | bytes 12292
  190.7 79.8 %copy-start.31 = (f32[768]{0:T(1024)}, f32[768]{0:T(1024)S(1)}, u32[]{:S(2)}) copy-start(f32[768]{0:T(1024)S(1)} %get-tuple-element.110) | copy-start | bytes 9220
  210.0 17.8 %copy-start.6 = (bf16[2,512,12,64]{1,0,3,2:T(2,128)(2,1)}, bf16[2,512,12,64]{1,0,3,2:T(2,128)(2,1)S(1)}, u32[]{:S(2)}) copy-start(bf16[2,512,12,64]{1,0,3,2:T(2,128)(2,1)S(1)} %reshape.346) | copy-start | bytes 4718596
  227.8 25.1 %copy-start.8 = (bf16[2,512,12,64]{1,0,3,2:T(2,128)(2,1)}, bf16[2,512,12,64]{1,0,3,2:T(2,128)(2,1)S(1)}, u32[]{:S(2)}) copy-start(bf16[2,512,12,64]{1,0,3,2:T(2,128)(2,1)S(1)} %reshape.344) | copy-start | bytes 4718596
  252.9 10.9 %copy-start.25 = (f32[2,12,512]{2,1,0:T(8,128)}, f32[2,12,512]{2,1,0:T(8,128)S(1)}, u32[]{:S(2)}) copy-start(f32[2,12,512]{2,1,0:T(8,128)S(1)} %log_add_fusion) | copy-start | bytes 147460
  265.9 4.0 copy-start.28
  271.9 8.1 copy-start.11
  279.9 75.3 %all-to-all-start.1 = ((bf16[8,256,768]{2,1,0:T(8,128)(2,1)}), bf16[8,256,768]{2,1,0:T(8,128)(2,1)S(1)}, u32[]{:S(2)}, u32[]{:S(2)}) async-start(bf16[8,256,768]{2,1,0:T(8,128)(2,1)} %bitcast.192), calls=%async_computation.1 | async-start | bytes 6291456 | tf_op jit(solution)/shard_map/all_to_all | solution.py:162
  359.0 33.8 %copy-start.2 = (bf16[2,8,128,768]{3,2,1,0:T(8,128)(2,1)}, bf16[2,8,128,768]{3,2,1,0:T(8,128)(2,1)S(1)}, u32[]{:S(2)}) copy-start(bf16[2,8,128,768]{3,2,1,0:T(8,128)(2,1)S(1)} %copy.295) | copy-start | bytes 9437188
  361.4 7.2 copy-start.15
  361.4 10.5 slice-start.5
  361.4 10.5 slice-start.6
  406.6 5.4 copy-start.55
  406.6 6.3 copy-start.30
  412.9 4.5 copy-start.57
  417.4 4.5 copy-start.16
  417.4 4.5 copy-start.23
  430.1 17.7 %slice-start.2 = ((s8[9437184]{0:T(1024)(128)(4,1)}), s8[4194304]{0:T(1024)(128)(4,1)S(1)}, s32[]{:S(2)}) async-start(s8[9437184]{0:T(1024)(128)(4,1)} %bitcast.208), calls=%async_computation.18 | async-start | bytes 8388608
  430.1 17.7 %slice-start.3 = ((s8[9437184]{0:T(1024)(128)(4,1)}), s8[4194304]{0:T(1024)(128)(4,1)S(1)}, s32[]{:S(2)}) async-start(s8[9437184]{0:T(1024)(128)(4,1)} %bitcast.208), calls=%async_computation.19 | async-start | bytes 8388608
  438.4 28.5 %copy-start.47 = (bf16[2,1024,768]{2,1,0:T(8,128)(2,1)}, bf16[2,1024,768]{2,1,0:T(8,128)(2,1)S(1)}, u32[]{:S(2)}) copy-start(bf16[2,1024,768]{2,1,0:T(8,128)(2,1)S(1)} %fusion.12) | copy-start | bytes 9437188
  438.4 9.5 slice-start.4
  447.9 23.6 %copy-start.48 = (bf16[2,1024,768]{2,1,0:T(8,128)(2,1)}, bf16[2,1024,768]{2,1,0:T(8,128)(2,1)S(1)}, u32[]{:S(2)}) copy-start(bf16[2,1024,768]{2,1,0:T(8,128)(2,1)S(1)} %fusion.19) | copy-start | bytes 9437188
  447.9 19.0 %slice-start.8 = ((s8[9437184]{0:T(1024)(128)(4,1)}), s8[4194304]{0:T(1024)(128)(4,1)S(1)}, s32[]{:S(2)}) async-start(s8[9437184]{0:T(1024)(128)(4,1)} %bitcast.221), calls=%async_computation.24 | async-start | bytes 8388608
  447.9 18.9 %slice-start.9 = ((s8[9437184]{0:T(1024)(128)(4,1)}), s8[4194304]{0:T(1024)(128)(4,1)S(1)}, s32[]{:S(2)}) async-start(s8[9437184]{0:T(1024)(128)(4,1)} %bitcast.221), calls=%async_computation.25 | async-start | bytes 8388608
  456.8 19.2 %copy-start.50 = (bf16[2,1024,768]{2,1,0:T(8,128)(2,1)}, bf16[2,1024,768]{2,1,0:T(8,128)(2,1)S(1)}, u32[]{:S(2)}) copy-start(bf16[2,1024,768]{2,1,0:T(8,128)(2,1)S(1)} %fusion.26) | copy-start | bytes 9437188
  456.8 10.0 slice-start.10
  476.0 4.5 copy-start.52
  496.8 75.1 %all-to-all-start.3 = ((bf16[8,256,768]{2,1,0:T(8,128)(2,1)}), bf16[8,256,768]{2,1,0:T(8,128)(2,1)S(1)}, u32[]{:S(2)}, u32[]{:S(2)}) async-start(bf16[8,256,768]{2,1,0:T(8,128)(2,1)} %bitcast.193), calls=%async_computation.3 | async-start | bytes 6291456 | tf_op jit(solution)/shard_map/all_to_all | solution.py:203
  573.6 75.1 %all-to-all-start.2 = ((bf16[8,256,768]{2,1,0:T(8,128)(2,1)}), bf16[8,256,768]{2,1,0:T(8,128)(2,1)S(1)}, u32[]{:S(2)}, u32[]{:S(2)}) async-start(bf16[8,256,768]{2,1,0:T(8,128)(2,1)} %bitcast.190), calls=%async_computation.2 | async-start | bytes 6291456 | tf_op jit(solution)/shard_map/all_to_all | solution.py:203
  577.2 4.7 copy-start.36
  577.2 255.6 %reduce-scatter.11.cloned.1.call-start = ((), (), s32[]{:S(2)}) async-start(), calls=%async_computation.10 | async-start | bytes 6144000 | tf_op jit(solution)/shard_map/reduce_scatter | solution.py:102
  584.6 5.7 copy-start.3
  584.6 5.7 copy-start.49
  648.7 8.3 copy-start.42
  666.5 4.5 copy-start.9
  666.5 4.5 copy-start.26
  700.9 25.7 %copy-start.10 = (bf16[2,512,12,64]{1,0,3,2:T(2,128)(2,1)S(1)}, bf16[2,512,12,64]{1,0,3,2:T(2,128)(2,1)}, u32[]{:S(2)}) copy-start(bf16[2,512,12,64]{1,0,3,2:T(2,128)(2,1)} %reshape.345) | copy-start | bytes 4718596
  726.6 8.6 copy-start.7
  735.2 6.9 copy-start.19
  735.2 6.9 copy-start.29
  749.8 7.1 slice-start
  751.2 5.7 slice-start.1
  776.1 117.7 %reduce-scatter.13.cloned.1.call-start = ((), (), s32[]{:S(2)}) async-start(), calls=%async_computation.13 | async-start | bytes 1382400
  832.9 132.5 %reduce-scatter.17.cloned.1.call-start = ((), (), s32[]{:S(2)}) async-start(), calls=%async_computation.15 | async-start | bytes 11796480
  833.7 229.9 %reduce-scatter.15.cloned.1.call-start = ((), (), s32[]{:S(2)}) async-start(), calls=%async_computation.14 | async-start | bytes 11796480
  863.2 22.3 %copy-start.20 = (f32[1024,768]{0,1:T(8,128)S(1)}, f32[1024,768]{0,1:T(8,128)}, u32[]{:S(2)}) copy-start(f32[1024,768]{0,1:T(8,128)} %copy-done.18) | copy-start | bytes 9437188
  863.2 22.3 %copy-start.24 = (f32[1024,768]{0,1:T(8,128)S(1)}, f32[1024,768]{0,1:T(8,128)}, u32[]{:S(2)}) copy-start(f32[1024,768]{0,1:T(8,128)} %get-tuple-element.153) | copy-start | bytes 9437188
  863.2 22.3 %copy-start.39 = (f32[1024]{0:T(1024)S(1)}, f32[1024]{0:T(1024)}, u32[]{:S(2)}) copy-start(f32[1024]{0:T(1024)} %get-tuple-element.129) | copy-start | bytes 12292
  870.9 1.2 collective-permute-start
  872.1 3.7 collective-permute-start.1
  875.7 4.5 collective-permute-start.2
  880.3 3.8 collective-permute-start.3
  884.1 9.1 collective-permute-start.4
  (22 other events, 47.6 us)
Sparse Core Ops, SparseCore 0:
  11.2 25.7 all-gather.6
  38.9 58.1 all-gather.8
  98.9 96.3 all-gather.10
  266.0 94.2 all-gather.12
  776.2 56.6 reduce-scatter.10
  835.0 33.7 reduce-scatter.12
  871.9 93.4 reduce-scatter.16
  968.5 95.0 reduce-scatter.14
